TPU v7x, 512 devices: a whole 4x8x8 slice. The times are simulated.
512 devices in a mesh: branch: 16 (over z, core), sub: 32 (over y, x).
Axes of the slice: x: 4, y: 8, z: 8, core: 2. Of those that a mesh axis runs over, the one named last changes fastest.
Arguments:
- sources: bfloat16 [64, 4194304], P(None, ('branch', 'sub')), may hold values from -6 to 6
- coords: bfloat16 [3, 4194304], P(None, ('branch', 'sub')), may hold values from 0 to 1
- leaf_basis: bfloat16 [16384, 64, 256], P(('branch', 'sub')), may hold values from -0.375 to 0.375
- leaf_transfer: float32 [16384, 64, 64], P(('branch', 'sub')), may hold values from -0.75 to 0.75
- cluster_transfer: float32 [512, 64, 64], P(('branch', 'sub'))
- near_slots: int32 [16384, 5], P(('branch', 'sub')), may hold values from 0 to 4, as said below
- near_count: int32 [16384], P(('branch', 'sub')), may hold values from 1 to 5, as said below
- cluster_partners: int32 [512, 6], P(('branch', 'sub')), may hold values from 0 to 31, as said below
- cluster_count: int32 [512], P(('branch', 'sub')), may hold values from 1 to 6, as said below
- cluster_coupling: float32 [512, 6, 64, 64], P(('branch', 'sub')), may hold values from -1.5 to 1.5
- branch_partners: int32 [16, 3], P('branch'), may hold values from 0 to 15, as said below
- branch_count: int32 [16], P('branch'), may hold values from 1 to 3, as said below
- branch_coupling_tiles: float32 [16, 3, 64, 64], P('branch'), may hold values from -1.5 to 1.5
Outputs:
- potential: float32 [64, 4194304], P(None, ('branch', 'sub'))
Inputs may be any that keep to these rules, and one draw needn't show every extreme that they name: `near_slots`: entry v of leaf i's row names leaf i + v - 2; each row holds every value once. Slot 0 holds 0 on the first leaf of each device's 32, and 4 on the last one (0 where they coincide). The first near_count[i] slots of leaf i are live. On every device all leaves have 5 live slots, or all have at most 2. `cluster_partners`: A row names 6 different device clusters of the same branch, never its own. The first cluster_count[d] slots of device cluster d are live. `branch_partners`: A row names 3 different branches, never its own. The first branch_count[b] slots of branch b are live.
All inputs are finite; a program needn't handle non-finite values.
Results may differ from a plain program's by a relative error of at most 0.0028.
Values may be sent and summed in bfloat16 or wider, within the bound.
A program may use at most 64 MiB of HBM per device.

v0:
```python
import jax
import jax.numpy as jnp
from jax import lax
from jax.sharding import PartitionSpec as P

LEAF = 256
COLS = 64
NEAR = 5
COUP = 6
BCOUP = 3
REACH = 2


KERNEL_SCALE = 0.03125
DELTA_SQUARED = 0.01


def extended(block, sides, width):
    for axis, dim in sides:
        count = lax.axis_size(axis)
        forward = [(i, i + 1) for i in range(count - 1)]
        backward = [(target, source) for source, target in forward]
        low = lax.ppermute(
            lax.slice_in_dim(block, block.shape[dim] - width, None, axis=dim), axis, forward
        )
        high = lax.ppermute(lax.slice_in_dim(block, 0, width, axis=dim), axis, backward)
        block = jnp.concatenate([low, block, high], axis=dim)
    return block


def kernel_batch(source_coords, target_coords):
    sources_f = source_coords.astype(jnp.float32)
    targets_f = target_coords.astype(jnp.float32)
    squared_distance = jnp.zeros(
        (sources_f.shape[1], sources_f.shape[2], targets_f.shape[2]), jnp.float32
    )
    for component in range(3):
        differ = sources_f[component][:, :, None] - targets_f[component][:, None, :]
        squared_distance = squared_distance + differ * differ
    return KERNEL_SCALE * lax.rsqrt(squared_distance + DELTA_SQUARED)


def solve_right_transposed(lower, values):
    return lax.linalg.triangular_solve(lower, values, left_side=False, lower=True, transpose_a=True)


def solve_right(lower, values):
    return lax.linalg.triangular_solve(
        lower, values, left_side=False, lower=True, transpose_a=False
    )


def couple_terms(blocks, partners, live_mask, tiles):
    count_here = blocks.shape[0]
    inside = jnp.logical_and(jnp.logical_and(partners >= 0, partners < count_here), live_mask)
    picked = blocks[jnp.clip(partners, 0, count_here - 1)]
    weights = inside.astype(jnp.float32)
    return jnp.einsum(
        "kcr,krs->cs", picked * weights[:, None, None], tiles, precision=lax.Precision.HIGHEST
    )


def shards(
    sources,
    coords,
    leaf_basis,
    leaf_transfer,
    cluster_transfer,
    near_slots,
    near_count,
    cluster_partners,
    cluster_count,
    cluster_coupling,
    branch_partners,
    branch_count,
    branch_coupling_tiles,
):
    highest = lax.Precision.HIGHEST
    margin = REACH * LEAF
    leaf_here = sources.shape[1] // LEAF
    packed = jnp.concatenate([sources, coords], axis=0)
    padded = extended(packed, ((("branch", "sub"), 1),), margin)
    padded_source_values = padded[:COLS]
    padded_coordinates = padded[COLS:]
    live = jnp.arange(NEAR, dtype=jnp.int32)[None, :] < near_count[:, None]
    window_sources = padded_source_values.reshape(COLS, leaf_here + 2 * REACH, LEAF)
    window_coords = padded_coordinates.reshape(3, leaf_here + 2 * REACH, LEAF)
    target_coords = coords.reshape(3, leaf_here, LEAF)
    live_f = live.astype(jnp.float32)
    near = jnp.zeros((COLS, leaf_here, LEAF), jnp.float32)
    for shift_value in range(NEAR):
        slot_weight = jnp.sum(jnp.where(near_slots == shift_value, live_f, 0.0), axis=1)
        shifted_coords = window_coords[:, shift_value : shift_value + leaf_here]
        shifted_values = window_sources[:, shift_value : shift_value + leaf_here]
        blocks = kernel_batch(shifted_coords, target_coords).astype(jnp.bfloat16)
        term = jnp.einsum(
            "clp,lpq->clq", shifted_values, blocks, preferred_element_type=jnp.float32
        )
        near = near + slot_weight[None, :, None] * term
    near = near.reshape(COLS, leaf_here * LEAF)
    leaf_values = sources.reshape(COLS, leaf_here, LEAF)
    leaf_up = jnp.einsum(
        "clp,lrp->lcr", leaf_values, leaf_basis, preferred_element_type=jnp.float32
    )
    leaf_gram = jnp.einsum(
        "lrp,lsp->lrs", leaf_basis, leaf_basis, preferred_element_type=jnp.float32
    )
    cluster_up = jnp.einsum("lcr,lrs->cs", leaf_up, leaf_transfer, precision=highest)
    half = jnp.einsum("lrt,ltu->lru", leaf_gram, leaf_transfer, precision=highest)
    cluster_gram = jnp.einsum("lrs,lru->su", leaf_transfer, half, precision=highest)
    cluster_lower = jnp.linalg.cholesky(cluster_gram)
    cluster_ortho = solve_right_transposed(cluster_lower, cluster_up)
    own_transfer = cluster_transfer[0]
    partners = cluster_partners[0]
    cluster_live = jnp.arange(COUP, dtype=jnp.int32) < cluster_count[0]
    tiles = cluster_coupling[0]
    cluster_out = couple_terms(
        lax.all_gather(cluster_ortho[None], "sub", axis=0, tiled=True),
        partners,
        cluster_live,
        tiles,
    )
    branch_up, branch_gram = (
        lax.psum(
            jnp.dot(cluster_ortho, own_transfer, precision=highest).astype(jnp.bfloat16), "sub"
        ).astype(jnp.float32),
        lax.psum(
            jnp.dot(own_transfer.T, own_transfer, precision=highest).astype(jnp.bfloat16), "sub"
        ).astype(jnp.float32),
    )
    branch_lower = jnp.linalg.cholesky(branch_gram)
    branch_ortho = solve_right_transposed(branch_lower, branch_up)
    branch_live = jnp.arange(BCOUP, dtype=jnp.int32) < branch_count[0]
    branch_tiles = branch_coupling_tiles[0]
    branch_ids = branch_partners[0]
    branch_out = couple_terms(
        lax.all_gather(branch_ortho[None], "branch", axis=0, tiled=True),
        branch_ids,
        branch_live,
        branch_tiles,
    )
    lifted = solve_right(branch_lower, branch_out)
    total_coeff = cluster_out + jnp.dot(lifted, own_transfer.T, precision=highest)
    down = solve_right(cluster_lower, total_coeff)
    leaf_down = jnp.einsum("cr,lqr->lcq", down, leaf_transfer, precision=highest).astype(
        jnp.bfloat16
    )
    far = jnp.einsum("lcq,lqp->clp", leaf_down, leaf_basis, preferred_element_type=jnp.float32)
    return near + far.reshape(COLS, leaf_here * LEAF)


def solution(mesh):
    return jax.shard_map(
        shards,
        mesh=mesh,
        in_specs=(
            P(None, ("branch", "sub")),
            P(None, ("branch", "sub")),
            P(("branch", "sub"), None, None),
            P(("branch", "sub"), None, None),
            P(("branch", "sub"), None, None),
            P(("branch", "sub"), None),
            P(("branch", "sub")),
            P(("branch", "sub"), None),
            P(("branch", "sub")),
            P(("branch", "sub"), None, None, None),
            P("branch", None),
            P("branch"),
            P("branch", None, None, None),
        ),
        out_specs=P(None, ("branch", "sub")),
        check_vma=False,
    )
```

profile of v0, /device:TPU:24, one launch (start us, length us, event | category | flops | bytes accessed | tf_op | source)
XLA Modules:
  0.0 326.3 jit_solution(4529692144436576347)
XLA Ops:
  0.0 1.4 constant_dynamic-update-slice_fusion.1
  1.4 0.0 copy-start.2
  1.4 0.7 fusion.94
  2.1 0.7 fusion.93
  2.8 3.4 %collective-permute-start = (bf16[67,512]{1,0:T(8,128)(2,1)}, bf16[67,512]{1,0:T(8,128)(2,1)S(1)}, u32[]{:S(2)}, u32[]{:S(2)}) collective-permute-start(bf16[67,512]{1,0:T(8,128)(2,1)} %get-tuple-element.23), channel_id=1, source_target_pairs={{0,1},{1,2},{2,3},{3,4},{4,5},{5,6},{6,7},{7,8},{8,9},{9,10},{10,1... | collective-permute-start | bytes 205832 | tf_op jit(solution)/shard_map/ppermute | solution.py:23
  6.2 4.6 %collective-permute-start.1 = (bf16[67,512]{1,0:T(8,128)(2,1)}, bf16[67,512]{1,0:T(8,128)(2,1)}, u32[]{:S(2)}, u32[]{:S(2)}) collective-permute-start(bf16[67,512]{1,0:T(8,128)(2,1)} %get-tuple-element.24), channel_id=1, source_target_pairs={{1,0},{2,1},{3,2},{4,3},{5,4},{6,5},{7,6},{8,7},{9,8},{10,9},{11,1... | collective-permute-start | bytes 205832 | tf_op jit(solution)/shard_map/ppermute | solution.py:26
  10.8 0.8 convolution_convert_fusion.2
  11.6 0.4 fusion.95
  12.0 0.0 copy-start.1
  12.0 0.4 fusion.47
  12.5 0.8 copy-done.1
  13.3 1.1 convolution_bitcast_fusion.5
  14.4 1.9 fusion.96
  16.3 0.0 copy-start.17
  16.3 0.0 copy-start.18
  16.3 1.1 fusion.97
  17.4 0.1 copy.34
  17.5 5.8 %cholesky.44 = f32[64,64]{1,0:T(8,128)S(1)} custom-call(f32[64,64]{1,0:T(8,128)S(1)} %fusion.63), custom_call_target="Cholesky" | custom-call | tf_op jit(solution)/shard_map/jit(cholesky)/cholesky | solution.py:111
  23.4 0.7 compare_reduce_fusion.1
  24.1 0.7 fusion.61
  24.8 4.9 %custom-call.13 = f32[1,64,64]{1,2,0:T(8,128)S(1)} custom-call(f32[1,64,64]{2,1,0:T(8,128)S(1)} %fusion.61), custom_call_target="InvertDiagBlocksLowerTriangular" | custom-call | tf_op jit(solution)/shard_map/triangular_solve/custom-call.2 | solution.py:48
  29.7 0.0 copy-start.5
  29.7 0.2 convolution_bitcast_fusion.4
  29.9 0.2 convolution_convert_fusion.1
  30.2 0.1 copy.36
  31.6 0.6 fusion.79
  32.2 0.6 fusion.78
  32.8 134.5 %all-reduce = (bf16[64,64]{0,1:T(8,128)(2,1)S(1)}, bf16[64,64]{1,0:T(8,128)(2,1)S(1)}) all-reduce(bf16[64,64]{0,1:T(8,128)(2,1)} %convolution_convert_fusion.2, bf16[64,64]{1,0:T(8,128)(2,1)S(1)} %convolution_convert_fusion.1), channel_id=1, replica_groups=mesh['branch'=16,'sub'=32] {'sub'}, use_global_device_ids=true, to_apply=%region_7.10 | all-reduce | flops 8192 | bytes 32768 | tf_op jit(solution)/shard_map/psum | solution.py:127
  167.3 0.1 copy.38
  167.4 5.8 %cholesky.55 = f32[64,64]{1,0:T(8,128)S(1)} custom-call(f32[64,64]{1,0:T(8,128)S(1)} %fusion.66), custom_call_target="Cholesky" | custom-call | tf_op jit(solution)/shard_map/jit(cholesky)/cholesky | solution.py:131
  173.3 0.6 compare_reduce_fusion
  174.0 0.7 fusion.62
  174.6 4.9 %custom-call.12 = f32[1,64,64]{1,2,0:T(8,128)S(1)} custom-call(f32[1,64,64]{2,1,0:T(8,128)S(1)} %fusion.62), custom_call_target="InvertDiagBlocksLowerTriangular" | custom-call | tf_op jit(solution)/shard_map/triangular_solve/custom-call.2 | solution.py:48
  179.5 0.3 convolution_bitcast_fusion.3
  179.8 0.1 copy.39
  179.9 26.0 %all-gather.1 = f32[1024,64]{1,0:T(8,128)} all-gather(f32[64,64]{1,0:T(8,128)S(1)} %copy.39), channel_id=3, replica_groups=mesh['branch'=16,'sub'=32] {'branch'}, dimensions={0}, use_global_device_ids=true | all-gather | bytes 278528 | tf_op jit(solution)/shard_map/all_gather | solution.py:137
  205.8 1.6 gather_fusion.1
  207.4 1.2 convolution_bitcast_fusion.2
  208.7 0.8 convolution_bitcast_fusion.1
  209.5 59.3 %all-gather = f32[2048,64]{1,0:T(8,128)} all-gather(f32[64,64]{1,0:T(8,128)S(1)} %copy.36), channel_id=2, replica_groups=mesh['branch'=16,'sub'=32] {'sub'}, dimensions={0}, use_global_device_ids=true | all-gather | bytes 540672 | tf_op jit(solution)/shard_map/all_gather | solution.py:118
  268.8 1.8 gather_fusion
  270.6 1.4 convolution_bitcast_fusion.6
  272.0 1.0 convolution_add_fusion
  273.0 0.9 convolution_bitcast_fusion
  274.0 3.9 %fusion.46 = bf16[32,64,64]{2,1,0:T(8,128)(2,1)} fusion(f32[64,64,1]{0,1,2:T(8,128)S(1)} %convolution_bitcast_fusion, f32[32,64,64]{2,1,0:T(8,128)S(1)} %copy-done.1), kind=kOutput, calls=%fused_computation.56 | convolution fusion | flops 100794368 | bytes 802816 | tf_op jit(solution)/shard_map/cr,lqr->lcq/dot_general | solution.py:145
  277.9 0.3 slice_reduce_fusion.2
  278.2 0.6 sub.104
  278.8 0.6 sub.219
  279.4 0.6 sub.214
  280.0 0.6 fusion.73
  280.6 0.7 pad_maximum_fusion.1
  281.3 0.7 reshape.149
  282.0 1.0 pad_maximum_fusion
  283.0 0.1 slice.157
  283.1 0.7 reshape.150
  283.8 1.1 slice_convert_fusion.4
  284.9 1.5 fusion.92
  286.5 7.4 %fusion = f32[32,256,64]{1,2,0:T(8,128)S(1)} fusion(f32[32,256]{1,0:T(8,128)S(1)} %copy-done.9, f32[32,256]{1,0:T(8,128)S(1)} %get-tuple-element.26, f32[32,256]{1,0:T(8,128)S(1)} %copy-done.10, f32[32,256]{1,0:T(8,128)S(1)} %get-tuple-element.27, f32[32,256]{1,0:T(8,128)S(1)} %copy-done.8, f32[32,256]{1,0:T(8,128)S(1)} %get-tuple-element.25, ...), kind=kOutput, calls=%fused_computation.7 | convolution fusion | flops 291504128 | bytes 3342336 | tf_op jit(solution)/shard_map/clp,lpq->clq/dot_general | solution.py:96
  293.9 7.4 %fusion.3 = f32[32,256,64]{1,2,0:T(8,128)S(1)} fusion(f32[32,256]{1,0:T(8,128)S(1)} %get-tuple-element.48, f32[32,256]{1,0:T(8,128)S(1)} %get-tuple-element.47, f32[32,256]{1,0:T(8,128)S(1)} %get-tuple-element.49, f32[32,256]{1,0:T(8,128)S(1)} %copy-done.9, f32[32,256]{1,0:T(8,128)S(1)} %copy-done.10, f32[32,256]{1,0:T(8,128)S(1)} %copy-done.8, ...), kind=kOutput, calls=%fused_computation.10 | convolution fusion | flops 291504128 | bytes 3342336 | tf_op jit(solution)/shard_map/clp,lpq->clq/dot_general | solution.py:96
  301.4 7.4 %fusion.2 = f32[32,256,64]{1,2,0:T(8,128)S(1)} fusion(f32[32,256]{1,0:T(8,128)S(1)} %get-tuple-element.32, f32[32,256]{1,0:T(8,128)S(1)} %get-tuple-element.33, f32[32,256]{1,0:T(8,128)S(1)} %get-tuple-element.31, f32[32,256]{1,0:T(8,128)S(1)} %copy-done.9, f32[32,256]{1,0:T(8,128)S(1)} %copy-done.10, f32[32,256]{1,0:T(8,128)S(1)} %copy-done.8, ...), kind=kOutput, calls=%fused_computation.9 | convolution fusion | flops 291504128 | bytes 3342336 | tf_op jit(solution)/shard_map/clp,lpq->clq/dot_general | solution.py:96
  308.8 7.4 %fusion.1 = f32[32,256,64]{1,2,0:T(8,128)S(1)} fusion(f32[32,256]{1,0:T(8,128)S(1)} %get-tuple-element.51, f32[32,256]{1,0:T(8,128)S(1)} %get-tuple-element.50, f32[32,256]{1,0:T(8,128)S(1)} %get-tuple-element.52, f32[32,256]{1,0:T(8,128)S(1)} %copy-done.9, f32[32,256]{1,0:T(8,128)S(1)} %copy-done.10, f32[32,256]{1,0:T(8,128)S(1)} %copy-done.8, ...), kind=kOutput, calls=%fused_computation.8 | convolution fusion | flops 291504128 | bytes 3342336 | tf_op jit(solution)/shard_map/clp,lpq->clq/dot_general | solution.py:96
  316.3 7.4 %fusion.4 = f32[32,256,64]{1,2,0:T(8,128)S(1)} fusion(f32[32,256]{1,0:T(8,128)S(1)} %get-tuple-element.38, f32[32,256]{1,0:T(8,128)S(1)} %get-tuple-element.39, f32[32,256]{1,0:T(8,128)S(1)} %get-tuple-element.37, f32[32,256]{1,0:T(8,128)S(1)} %copy-done.9, f32[32,256]{1,0:T(8,128)S(1)} %copy-done.10, f32[32,256]{1,0:T(8,128)S(1)} %copy-done.8, ...), kind=kOutput, calls=%fused_computation.11 | convolution fusion | flops 291504128 | bytes 3342336 | tf_op jit(solution)/shard_map/clp,lpq->clq/dot_general | solution.py:96
  323.7 1.1 fusion.45
  324.8 1.5 copy.52
  (45 shorter events, 0.2 us)
Async XLA Ops:
  0.0 11.6 %copy-start = (bf16[32,64,256]{2,1,0:T(8,128)(2,1)S(1)}, bf16[32,64,256]{2,1,0:T(8,128)(2,1)}, u32[]{:S(2)}) copy-start(bf16[32,64,256]{2,1,0:T(8,128)(2,1)} %param.20) | copy-start | bytes 3145732
  0.0 1.4 copy-start.7
  0.0 10.7 %copy-start.6 = (f32[1,64,64]{2,1,0:T(8,128)S(1)}, f32[1,64,64]{2,1,0:T(8,128)}, u32[]{:S(2)}) copy-start(f32[1,64,64]{2,1,0:T(8,128)} %param.22) | copy-start | bytes 49156
  1.4 10.6 %copy-start.2 = (bf16[64,8192]{1,0:T(8,128)(2,1)S(1)}, bf16[64,8192]{1,0:T(8,128)(2,1)}, u32[]{:S(2)}) copy-start(bf16[64,8192]{1,0:T(8,128)(2,1)} %param.18) | copy-start | bytes 3145732
  2.8 277.8 %collective-permute-start = (bf16[67,512]{1,0:T(8,128)(2,1)}, bf16[67,512]{1,0:T(8,128)(2,1)S(1)}, u32[]{:S(2)}, u32[]{:S(2)}) collective-permute-start(bf16[67,512]{1,0:T(8,128)(2,1)} %get-tuple-element.23), channel_id=1, source_target_pairs={{0,1},{1,2},{2,3},{3,4},{4,5},{5,6},{6,7},{7,8},{8,9},{9,10},{10,1... | collective-permute-start | bytes 205832 | tf_op jit(solution)/shard_map/ppermute | solution.py:23
  6.2 274.4 %collective-permute-start.1 = (bf16[67,512]{1,0:T(8,128)(2,1)}, bf16[67,512]{1,0:T(8,128)(2,1)}, u32[]{:S(2)}, u32[]{:S(2)}) collective-permute-start(bf16[67,512]{1,0:T(8,128)(2,1)} %get-tuple-element.24), channel_id=1, source_target_pairs={{1,0},{2,1},{3,2},{4,3},{5,4},{6,5},{7,6},{8,7},{9,8},{10,9},{11,1... | collective-permute-start | bytes 205832 | tf_op jit(solution)/shard_map/ppermute | solution.py:26
  12.0 1.2 copy-start.1
  16.3 15.3 %copy-start.17 = (s32[1,6]{1,0:T(1,128)S(1)}, s32[1,6]{1,0:T(1,128)}, u32[]{:S(2)}) copy-start(s32[1,6]{1,0:T(1,128)} %param.25) | copy-start | bytes 76
  16.3 15.9 %copy-start.18 = (s32[1,3]{1,0:T(1,128)S(1)}, s32[1,3]{1,0:T(1,128)}, u32[]{:S(2)}) copy-start(s32[1,3]{1,0:T(1,128)} %param.28) | copy-start | bytes 40
  29.7 176.2 %copy-start.5 = (f32[1,64,64]{1,2,0:T(8,128)}, f32[1,64,64]{1,2,0:T(8,128)S(1)}, u32[]{:S(2)}) copy-start(f32[1,64,64]{1,2,0:T(8,128)S(1)} %custom-call.13) | copy-start | bytes 49156
  208.7 71.3 %copy-start.11 = (s32[32,5]{0,1:T(8,128)S(1)}, s32[32,5]{0,1:T(8,128)}, u32[]{:S(2)}) copy-start(s32[32,5]{0,1:T(8,128)} %param.23) | copy-start | bytes 1924
  270.6 7.3 %copy-start.4 = (f32[3,8192]{1,0:T(4,128)S(1)}, f32[3,8192]{1,0:T(4,128)}, u32[]{:S(2)}) copy-start(f32[3,8192]{1,0:T(4,128)} %get-tuple-element.40) | copy-start | bytes 294916
  272.0 8.0 %copy-start.16 = (s32[32]{0:T(128)S(1)}, s32[32]{0:T(128)}, u32[]{:S(2)}) copy-start(s32[32]{0:T(128)} %param.24) | copy-start | bytes 388
  284.9 1.6 copy-start.8
  284.9 1.6 copy-start.9
  284.9 1.6 copy-start.10
  316.2 7.5 %copy-start.3 = (bf16[32,64,64]{2,1,0:T(8,128)(2,1)S(1)}, bf16[32,64,64]{2,1,0:T(8,128)(2,1)}, u32[]{:S(2)}) copy-start(bf16[32,64,64]{2,1,0:T(8,128)(2,1)} %fusion.46) | copy-start | bytes 786436
  316.2 7.5 %copy-start.12 = (f32[32]{0:T(128)S(1)}, f32[32]{0:T(128)}, u32[]{:S(2)}) copy-start(f32[32]{0:T(128)} %get-tuple-element.12) | copy-start | bytes 388
  316.2 7.5 %copy-start.13 = (f32[32]{0:T(128)S(1)}, f32[32]{0:T(128)}, u32[]{:S(2)}) copy-start(f32[32]{0:T(128)} %get-tuple-element.13) | copy-start | bytes 388
  316.3 7.5 %copy-start.14 = (f32[32]{0:T(128)S(1)}, f32[32]{0:T(128)}, u32[]{:S(2)}) copy-start(f32[32]{0:T(128)} %get-tuple-element.14) | copy-start | bytes 388
  316.3 7.5 %copy-start.15 = (f32[32]{0:T(128)S(1)}, f32[32]{0:T(128)}, u32[]{:S(2)}) copy-start(f32[32]{0:T(128)} %get-tuple-element.15) | copy-start | bytes 388
where the time goes:
time: 327 us; the launch traced here: 326 us
  blocking collectives  220 us (67%)
  matrix products  54 us (17%)
  other arithmetic  29.6 us (9%)
  local copies, waits for them, and re-layouts  13.2 us (4%)
  starting transfers between devices  7.94 us (2%)
    psum x1, blocking collectives, shards(): lax.psum(jnp.dot(own_transfer.T, own_transfer, precision=highest).astype(...  135 us
    all_gather x1, blocking collectives, shards(): lax.all_gather(cluster_ortho[None], 'sub', axis=0, tiled=True)  59.3 us
    dot_general x5, matrix products, shards(): jnp.einsum('clp,lpq->clq', shifted_values, blocks, preferred_element_type...  37.1 us
    all_gather x1, blocking collectives, shards(): lax.all_gather(branch_ortho[None], 'branch', axis=0, tiled=True)  26 us
    another operation x4, other arithmetic, solve_right(): lax.linalg.triangular_solve(lower, values, left_side=False, lower=True, t...  11.1 us
    another operation x3, other arithmetic, shards(): cluster_lower = jnp.linalg.cholesky(cluster_gram)  6.6 us
  transfers between devices with their start and end apart: 2, of which 0 were waited for; matrix products, arithmetic and copies ran while one was open for 15% of the time, Pallas kernels for 0%

commit v1 on v0

v1 whole, which is shorter than its diff:
```python
import functools

import jax
import jax.numpy as jnp
from jax import lax
from jax.experimental import pallas as pl
from jax.experimental.pallas import tpu as pltpu
from jax.sharding import PartitionSpec as P

LEAF = 256
RANK = 64
COLS = 64
HERE = 32
NEAR = 5
COUP = 6
BCOUP = 3
REACH = 2
MARGIN = REACH * LEAF
POINTS = HERE * LEAF
PADDED = POINTS + 2 * MARGIN
FEAT = 16

KERNEL_SCALE = 0.03125
DELTA_SQUARED = 0.01

NX, NY = 4, 8
NZ, NC = 8, 2
N_SUB = NX * NY
N_BRANCH = NZ * NC

HIGHEST = lax.Precision.HIGHEST
MESH = pl.DeviceIdType.MESH
F32 = jnp.float32
BF16 = jnp.bfloat16

CHOL_LEAVES = 16
CHOL_STEPS = RANK // CHOL_LEAVES


def dot_nn(a, b, precision=None):
    return lax.dot_general(
        a, b, (((1,), (0,)), ((), ())), precision=precision, preferred_element_type=F32
    )


def dot_nt(a, b, precision=None):
    return lax.dot_general(
        a, b, (((1,), (1,)), ((), ())), precision=precision, preferred_element_type=F32
    )


def packed(x):
    half = x.shape[0] // 2
    return jnp.concatenate([x[:half], x[half:]], axis=1)


def unpacked(x):
    half = x.shape[1] // 2
    return jnp.concatenate([x[:, :half], x[:, half:]], axis=0)


def diagonal_blocks(x):
    return x[:RANK, :RANK] + x[RANK:, RANK:]


def features(coords):
    c = coords.astype(F32)
    x, y, z = c[0:1], c[1:2], c[2:3]
    norm = x * x + y * y + z * z + 0.5 * DELTA_SQUARED
    n1 = norm.astype(BF16).astype(F32)
    n2 = (norm - n1).astype(BF16).astype(F32)
    n3 = norm - n1 - n2
    row = lax.broadcasted_iota(jnp.int32, (FEAT, coords.shape[1]), 0)
    ones = jnp.ones_like(norm)

    def stacked(parts):
        out = jnp.zeros((FEAT, coords.shape[1]), F32)
        for at, part in enumerate(parts):
            out = jnp.where(row == at, part, out)
        return out.astype(BF16)

    source = stacked([x, y, z, n1, n2, n3, ones, ones, ones])
    target = stacked([-2.0 * x, -2.0 * y, -2.0 * z, ones, ones, ones, n1, n2, n3])
    return source, target


def eliminate(k, left, right):
    for ref in (left, right):
        square = ref[:, 0:128]
        lane = lax.broadcasted_iota(jnp.int32, square.shape, 1)
        row = lax.broadcasted_iota(jnp.int32, (RANK, 1), 0)
        column = jnp.sum(jnp.where(lane == k, square, 0.0), axis=1, keepdims=True)
        pivot_row = ref[pl.ds(k, 1), :]
        lane_row = lax.broadcasted_iota(jnp.int32, pivot_row.shape, 1)
        pivot = jnp.sum(jnp.where(lane_row == k, pivot_row, 0.0), axis=1, keepdims=True)
        factor = jnp.where(row > k, column * (1.0 / pivot), 0.0)
        ref[...] = ref[...] - factor * pivot_row


def row_scale(square):
    row = lax.broadcasted_iota(jnp.int32, (RANK, 128), 0)
    lane = lax.broadcasted_iota(jnp.int32, (RANK, 128), 1)
    pivots = jnp.sum(jnp.where(row == lane, square, 0.0), axis=1, keepdims=True)
    return lax.rsqrt(pivots)


def main_kernel(
    sources,
    coords,
    basis_hbm,
    transfer_hbm,
    cluster_transfer,
    near_slots,
    near_count,
    cluster_partners,
    cluster_count,
    coupling,
    branch_partners,
    branch_count,
    branch_tiles,
    near_out,
    vt_out,
    down_out,
    basis,
    transfer,
    window,
    source_feat,
    target_feat,
    source_feat_t,
    all_transfer,
    all_transfer_t,
    all_ortho,
    all_branch,
    left,
    right,
    local_sems,
    halo_send,
    halo_recv,
    send_sems,
    recv_sems,
):
    branch = lax.axis_index("branch")
    sub = lax.axis_index("sub")
    sx, sy = sub % NX, sub // NX
    bz, bc = branch // NC, branch % NC

    load_basis = pltpu.make_async_copy(basis_hbm, basis, local_sems.at[0])
    load_transfer = pltpu.make_async_copy(transfer_hbm, transfer, local_sems.at[1])
    load_sources = pltpu.make_async_copy(
        sources, window.at[:, pl.ds(MARGIN, POINTS)], local_sems.at[2]
    )
    load_basis.start()
    load_transfer.start()
    load_sources.start()

    def sub_peer(o):
        return ((sy + o // NX) % NY) * NX + (sx + o % NX) % NX

    def branch_peer(o):
        return ((bz + o // NC) % NZ) * NC + (bc + o % NC) % NC

    here = branch * N_SUB + sub
    total = N_BRANCH * N_SUB
    after = (here + 1) % total
    before = (here + total - 1) % total
    after_id = (after // N_SUB, after % N_SUB)
    before_id = (before // N_SUB, before % N_SUB)

    barrier = pltpu.get_barrier_semaphore()

    @pl.loop(1, N_SUB)
    def _(o):
        pl.semaphore_signal(
            barrier, inc=1, device_id=(branch, sub_peer(o)), device_id_type=MESH
        )

    @pl.loop(1, N_BRANCH)
    def _(o):
        pl.semaphore_signal(
            barrier, inc=1, device_id=(branch_peer(o), sub), device_id_type=MESH
        )

    pl.semaphore_signal(barrier, inc=1, device_id=after_id, device_id_type=MESH)
    pl.semaphore_signal(barrier, inc=1, device_id=before_id, device_id_type=MESH)

    own_transfer = cluster_transfer[0]
    all_transfer[0] = packed(own_transfer).astype(BF16)
    feat_source, feat_target = features(coords[...])
    source_feat[:, MARGIN : MARGIN + POINTS] = feat_source
    target_feat[...] = feat_target

    pl.semaphore_wait(barrier, N_SUB - 1 + N_BRANCH - 1 + 2)

    def sub_copy(buffer, slot, o):
        return pltpu.make_async_remote_copy(
            src_ref=buffer.at[0],
            dst_ref=buffer.at[o],
            send_sem=send_sems.at[slot],
            recv_sem=recv_sems.at[slot],
            device_id=(branch, sub_peer(o)),
            device_id_type=MESH,
        )

    def all_copies(buffer, slot, count):
        return pltpu.make_async_remote_copy(
            src_ref=buffer.at[pl.ds(1, count - 1)],
            dst_ref=buffer.at[pl.ds(1, count - 1)],
            send_sem=send_sems.at[slot],
            recv_sem=recv_sems.at[slot],
            device_id=(branch, sub_peer(1)),
            device_id_type=MESH,
        )

    @pl.loop(1, N_SUB)
    def _(o):
        sub_copy(all_transfer, 0, o).start()

    def halo_copy(src, dst, at, device):
        return pltpu.make_async_remote_copy(
            src_ref=src,
            dst_ref=dst,
            send_sem=halo_send.at[at],
            recv_sem=halo_recv.at[at],
            device_id=device,
            device_id_type=MESH,
        )

    low, high = pl.ds(0, MARGIN), pl.ds(MARGIN + POINTS, MARGIN)
    halos = [
        halo_copy(
            sources.at[:, pl.ds(POINTS - MARGIN, MARGIN)], window.at[:, low], 0, after_id
        ),
        halo_copy(sources.at[:, pl.ds(0, MARGIN)], window.at[:, high], 1, before_id),
        halo_copy(
            source_feat.at[:, pl.ds(POINTS, MARGIN)], source_feat.at[:, low], 2, after_id
        ),
        halo_copy(
            source_feat.at[:, pl.ds(MARGIN, MARGIN)], source_feat.at[:, high], 3, before_id
        ),
    ]
    for copy in halos:
        copy.start()

    def transpose_features(at):
        columns = pl.ds(pl.multiple_of(at * LEAF, LEAF), LEAF)
        block = source_feat[:, columns].astype(F32)
        source_feat_t[columns, :] = block.T.astype(BF16)

    @pl.loop(REACH, REACH + HERE)
    def _(at):
        transpose_features(at)

    load_basis.wait()
    load_transfer.wait()
    load_sources.wait()

    def climb(at, total_up):
        columns = pl.ds(pl.multiple_of(at * LEAF, LEAF), LEAF)
        block = transfer[at].T
        block_high = block.astype(BF16)
        block_low = (block - block_high.astype(F32)).astype(BF16)
        leaf_basis = basis[at]
        vt = (dot_nn(block_high, leaf_basis) + dot_nn(block_low, leaf_basis)).astype(BF16)
        vt_out[:, columns] = vt
        values = window[:, pl.ds(pl.multiple_of(MARGIN + at * LEAF, LEAF), LEAF)]
        return total_up + dot_nt(vt, jnp.concatenate([vt, values], axis=0))

    gram_up = lax.fori_loop(0, HERE, climb, jnp.zeros((RANK, 2 * RANK), F32), unroll=4)
    row = lax.broadcasted_iota(jnp.int32, (RANK, 128), 0)
    lane = lax.broadcasted_iota(jnp.int32, (RANK, 128), 1)
    left[:, 0:128] = gram_up
    left[:, 128:256] = jnp.where(row == lane, 1.0, 0.0)

    all_copies(all_transfer, 0, N_SUB).wait_recv()
    stack = all_transfer[...].reshape(N_SUB * RANK // 2, 2 * RANK)
    stack_t = stack.astype(F32).T.astype(BF16)
    all_transfer_t[...] = stack_t
    branch_gram = diagonal_blocks(dot_nn(stack_t, stack))
    right[...] = jnp.concatenate(
        [branch_gram, jnp.where(row == lane, 1.0, 0.0)[:, :RANK]], axis=1
    )

    def near_leaf(at):
        target = target_feat[:, pl.ds(pl.multiple_of(at * LEAF, LEAF), LEAF)]
        live = near_count[at]
        result = jnp.zeros((COLS, LEAF), F32)
        for shift in range(NEAR):
            weight = jnp.int32(0)
            for slot in range(NEAR):
                weight = weight + jnp.where(
                    jnp.logical_and(near_slots[at, slot] == shift, slot < live), 1, 0
                )
            points = pl.ds(pl.multiple_of((at + shift) * LEAF, LEAF), LEAF)
            distance = dot_nn(source_feat_t[points, :], target)
            block = lax.rsqrt(distance).astype(BF16)
            values = window[:, points]
            values = values * jnp.full(values.shape, weight.astype(F32)).astype(BF16)
            result = result + dot_nn(values, block)
        near_out[:, pl.ds(pl.multiple_of(at * LEAF, LEAF), LEAF)] = result * KERNEL_SCALE

    @pl.loop(0, CHOL_LEAVES)
    def _(it):
        near_leaf(it + REACH)
        for j in range(CHOL_STEPS):
            eliminate(it * CHOL_STEPS + j, left, right)

    scale = row_scale(left[:, 0:128])
    ortho_t = left[:, RANK : 2 * RANK] * scale
    all_ortho[0] = packed(ortho_t).astype(BF16)

    @pl.loop(1, N_SUB)
    def _(o):
        sub_copy(all_ortho, 1, o).start()

    inverse = left[:, 128 : 128 + RANK] * scale
    inverse_t = inverse.T
    branch_inverse = right[:, RANK:] * row_scale(right[...])
    cluster_map = dot_nt(inverse_t, coupling[0].reshape(COUP * RANK, RANK), HIGHEST)
    handed = dot_nt(dot_nn(inverse_t, own_transfer, HIGHEST), branch_inverse, HIGHEST)
    branch_map = dot_nt(handed, branch_tiles[0].reshape(BCOUP * RANK, RANK), HIGHEST)

    @pl.loop(REACH + CHOL_LEAVES, HERE - REACH)
    def _(at):
        near_leaf(at)

    all_copies(all_ortho, 1, N_SUB).wait_recv()
    branch_up_t = diagonal_blocks(
        dot_nn(all_transfer_t[...], all_ortho[...].reshape(N_SUB * RANK // 2, 2 * RANK))
    )
    branch_ortho_t = dot_nn(branch_inverse, branch_up_t, HIGHEST)
    all_branch[0] = packed(branch_ortho_t).astype(BF16)

    @pl.loop(1, N_BRANCH)
    def _(o):
        pltpu.make_async_remote_copy(
            src_ref=all_branch.at[0],
            dst_ref=all_branch.at[o],
            send_sem=send_sems.at[2],
            recv_sem=recv_sems.at[2],
            device_id=(branch_peer(o), sub),
            device_id_type=MESH,
        ).start()

    picked = []
    for k in range(COUP):
        partner = cluster_partners[0, k]
        slot = ((sy - partner // NX + NY) % NY) * NX + (sx - partner % NX + NX) % NX
        alive = jnp.where(k < cluster_count[0], 1.0, 0.0)
        picked.append(unpacked(all_ortho[slot].astype(F32)) * alive)
    down_t = dot_nn(cluster_map, jnp.concatenate(picked, axis=0), HIGHEST)

    for copy in halos:
        copy.wait_recv()
    keep_low = jnp.where(here == 0, 0.0, 1.0)
    keep_high = jnp.where(here == total - 1, 0.0, 1.0)
    for columns, keep in ((slice(0, MARGIN), keep_low), (slice(MARGIN + POINTS, PADDED), keep_high)):
        edge = window[:, columns]
        window[:, columns] = edge * jnp.full(edge.shape, keep).astype(BF16)
    for at in (0, 1, HERE + REACH, HERE + REACH + 1):
        transpose_features(at)

    @pl.loop(0, 2 * REACH)
    def _(it):
        near_leaf(jnp.where(it < REACH, it, HERE - 2 * REACH + it))

    all_copies(all_branch, 2, N_BRANCH).wait_recv()
    picked = []
    for k in range(BCOUP):
        partner = branch_partners[0, k]
        slot = ((bz - partner // NC + NZ) % NZ) * NC + (bc - partner % NC + NC) % NC
        alive = jnp.where(k < branch_count[0], 1.0, 0.0)
        picked.append(unpacked(all_branch[slot].astype(F32)) * alive)
    down_t = down_t + dot_nn(branch_map, jnp.concatenate(picked, axis=0), HIGHEST)
    down_out[...] = down_t.T

    for copy in halos:
        copy.wait_send()
    all_copies(all_transfer, 0, N_SUB).wait_send()
    all_copies(all_ortho, 1, N_SUB).wait_send()
    all_copies(all_branch, 2, N_BRANCH).wait_send()


def far_kernel(near, vt, down, out):
    high = down[...].astype(BF16)
    low = (down[...] - high.astype(F32)).astype(BF16)
    out[...] = near[...] + dot_nn(high, vt[...]) + dot_nn(low, vt[...])


def shards(
    sources,
    coords,
    leaf_basis,
    leaf_transfer,
    cluster_transfer,
    near_slots,
    near_count,
    cluster_partners,
    cluster_count,
    cluster_coupling,
    branch_partners,
    branch_count,
    branch_coupling_tiles,
):
    vmem = pl.BlockSpec(memory_space=pltpu.VMEM)
    smem = pl.BlockSpec(memory_space=pltpu.SMEM)
    hbm = pl.BlockSpec(memory_space=pl.ANY)
    near, vt, down = pl.pallas_call(
        main_kernel,
        out_shape=(
            jax.ShapeDtypeStruct((COLS, POINTS), F32),
            jax.ShapeDtypeStruct((RANK, POINTS), BF16),
            jax.ShapeDtypeStruct((COLS, RANK), F32),
        ),
        in_specs=[
            hbm,
            vmem,
            hbm,
            hbm,
            vmem,
            smem,
            smem,
            smem,
            smem,
            vmem,
            smem,
            smem,
            vmem,
        ],
        out_specs=(vmem, vmem, vmem),
        scratch_shapes=[
            pltpu.VMEM((HERE, RANK, LEAF), BF16),
            pltpu.VMEM((HERE, RANK, RANK), F32),
            pltpu.VMEM((COLS, PADDED), BF16),
            pltpu.VMEM((FEAT, PADDED), BF16),
            pltpu.VMEM((FEAT, POINTS), BF16),
            pltpu.VMEM((PADDED, FEAT), BF16),
            pltpu.VMEM((N_SUB, RANK // 2, 2 * RANK), BF16),
            pltpu.VMEM((2 * RANK, N_SUB * RANK // 2), BF16),
            pltpu.VMEM((N_SUB, RANK // 2, 2 * RANK), BF16),
            pltpu.VMEM((N_BRANCH, RANK // 2, 2 * RANK), BF16),
            pltpu.VMEM((RANK, 256), F32),
            pltpu.VMEM((RANK, 128), F32),
            pltpu.SemaphoreType.DMA((3,)),
            pltpu.SemaphoreType.DMA((4,)),
            pltpu.SemaphoreType.DMA((4,)),
            pltpu.SemaphoreType.DMA((3,)),
            pltpu.SemaphoreType.DMA((3,)),
        ],
        compiler_params=pltpu.CompilerParams(
            collective_id=0, has_side_effects=True, vmem_limit_bytes=40 * 2**20
        ),
        name="h2_main",
    )(
        sources,
        coords,
        leaf_basis,
        leaf_transfer,
        cluster_transfer,
        near_slots,
        near_count,
        cluster_partners,
        cluster_count,
        cluster_coupling,
        branch_partners,
        branch_count,
        branch_coupling_tiles,
    )
    chunk = 2048
    return pl.pallas_call(
        far_kernel,
        out_shape=jax.ShapeDtypeStruct((COLS, POINTS), F32),
        grid=(POINTS // chunk,),
        in_specs=[
            pl.BlockSpec((COLS, chunk), lambda i: (0, i)),
            pl.BlockSpec((RANK, chunk), lambda i: (0, i)),
            pl.BlockSpec((COLS, RANK), lambda i: (0, 0)),
        ],
        out_specs=pl.BlockSpec((COLS, chunk), lambda i: (0, i)),
        compiler_params=pltpu.CompilerParams(vmem_limit_bytes=32 * 2**20),
        name="h2_far",
    )(near, vt, down)


def solution(mesh):
    return jax.shard_map(
        shards,
        mesh=mesh,
        in_specs=(
            P(None, ("branch", "sub")),
            P(None, ("branch", "sub")),
            P(("branch", "sub"), None, None),
            P(("branch", "sub"), None, None),
            P(("branch", "sub"), None, None),
            P(("branch", "sub"), None),
            P(("branch", "sub")),
            P(("branch", "sub"), None),
            P(("branch", "sub")),
            P(("branch", "sub"), None, None, None),
            P("branch", None),
            P("branch"),
            P("branch", None, None, None),
        ),
        out_specs=P(None, ("branch", "sub")),
        check_vma=False,
    )
```

time: 327 us -> 71.4 us (0.22)
  the two profiles are of different devices: /device:TPU:24 before, /device:TPU:1 now
where the time goes in v1:
time: 71.4 us; the launch traced here: 71 us
  Pallas kernels  59.8 us (84%)
  local copies, waits for them, and re-layouts  9.82 us (14%)
  between operations  1.32 us (2%)
    pallas_call x1, Pallas kernels, shards(): pl.pallas_call(main_kernel, out_shape=(jax.ShapeDtypeStruct((COLS, POINTS...  57.2 us
    unnamed x21, local copies, waits for them, and re-layouts  9.82 us
    pallas_call x1, Pallas kernels, shards(): pl.pallas_call(far_kernel, out_shape=jax.ShapeDtypeStruct((COLS, POINTS),...  2.63 us

profile of v1, /device:TPU:1, one launch (start us, length us, event | category | flops | bytes accessed | tf_op | source)
XLA Modules:
  0.0 71.0 jit_solution(11939975998186324572)
XLA Ops:
  1.3 0.8 %copy.14.near_slots = s32[32,5]{1,0:T(8,128)S(1)} copy(s32[32,5]{0,1:T(8,128)} %param.18) | data formatting | bytes 1280 | tf_op args[5]
  2.1 0.0 copy-start
  2.1 1.2 %copy-done = bf16[64,8192]{1,0:T(8,128)(2,1)S(1)} copy-done((bf16[64,8192]{1,0:T(8,128)(2,1)S(1)}, bf16[64,8192]{1,0:T(8,128)(2,1)}, u32[]{:S(2)}) %copy-start) | copy-done | bytes 1048600
  3.3 0.0 copy-start.1
  3.3 1.2 %copy-done.1 = bf16[32,64,256]{2,1,0:T(8,128)(2,1)S(1)} copy-done((bf16[32,64,256]{2,1,0:T(8,128)(2,1)S(1)}, bf16[32,64,256]{2,1,0:T(8,128)(2,1)}, u32[]{:S(2)}) %copy-start.1) | copy-done | bytes 1048600
  4.5 0.0 copy-start.2
  4.5 1.2 %copy-done.2 = f32[32,64,64]{2,1,0:T(8,128)S(1)} copy-done((f32[32,64,64]{2,1,0:T(8,128)S(1)}, f32[32,64,64]{2,1,0:T(8,128)}, u32[]{:S(2)}) %copy-start.2) | copy-done | bytes 524312
  5.7 0.0 copy-start.3
  5.7 0.9 %copy-done.3 = f32[1,6,64,64]{3,2,1,0:T(8,128)S(1)} copy-done((f32[1,6,64,64]{3,2,1,0:T(8,128)S(1)}, f32[1,6,64,64]{3,2,1,0:T(8,128)}, u32[]{:S(2)}) %copy-start.3) | copy-done | bytes 98328
  6.7 0.0 copy-start.4
  6.7 0.9 %copy-done.4 = f32[1,3,64,64]{3,2,1,0:T(8,128)S(1)} copy-done((f32[1,3,64,64]{3,2,1,0:T(8,128)S(1)}, f32[1,3,64,64]{3,2,1,0:T(8,128)}, u32[]{:S(2)}) %copy-start.4) | copy-done | bytes 49176
  7.6 0.0 copy-start.5
  7.6 0.8 %copy-done.5 = bf16[3,8192]{1,0:T(4,128)(2,1)S(1)} copy-done((bf16[3,8192]{1,0:T(4,128)(2,1)S(1)}, bf16[3,8192]{1,0:T(4,128)(2,1)}, u32[]{:S(2)}) %copy-start.5) | copy-done | bytes 49176
  8.4 0.0 copy-start.6
  8.4 0.8 %copy-done.6 = f32[1,64,64]{2,1,0:T(8,128)S(1)} copy-done((f32[1,64,64]{2,1,0:T(8,128)S(1)}, f32[1,64,64]{2,1,0:T(8,128)}, u32[]{:S(2)}) %copy-start.6) | copy-done | bytes 16408
  9.2 0.0 copy-start.7
  9.2 0.7 copy-done.7
  9.8 0.0 copy-start.8
  9.8 0.7 copy-done.8
  10.5 0.0 copy-start.9
  10.5 0.7 copy-done.9
  11.1 57.2 %h2_main.1 = (f32[64,8192]{1,0:T(8,128)S(1)}, bf16[64,8192]{1,0:T(8,128)(2,1)S(1)}, f32[64,64]{1,0:T(8,128)S(1)}) custom-call(bf16[64,8192]{1,0:T(8,128)(2,1)S(1)} %copy-done, bf16[3,8192]{1,0:T(4,128)(2,1)S(1)} %copy-done.5, bf16[32,64,256]{2,1,0:T(8,128)(2,1)S(1)} %copy-done.1, f32[32,64,64]{2,1,0:T(8,128)S(1)} %copy-done.2, f32[1,64,64]{2,1,0:T(8,128)S(1)} %copy-done.6, ...), custom_call_target="tpu_custom_call" | custom-call | tf_op jit(solution)/shard_map/h2_main/pallas_call | solution.py:407
  68.3 2.6 %h2_far.1 = f32[64,8192]{1,0:T(8,128)} custom-call(f32[64,8192]{1,0:T(8,128)S(1)} %get-tuple-element.8.near, bf16[64,8192]{1,0:T(8,128)(2,1)S(1)} %get-tuple-element.9.vt, f32[64,64]{1,0:T(8,128)S(1)} %get-tuple-element.10.down), custom_call_target="tpu_custom_call" | custom-call | tf_op jit(solution)/shard_map/h2_far/pallas_call | solution.py:469
Async XLA Ops:
  2.1 1.2 %copy-start = (bf16[64,8192]{1,0:T(8,128)(2,1)S(1)}, bf16[64,8192]{1,0:T(8,128)(2,1)}, u32[]{:S(2)}) copy-start(bf16[64,8192]{1,0:T(8,128)(2,1)} %sources.1) | copy-start | bytes 3145732
  3.3 1.2 %copy-start.1 = (bf16[32,64,256]{2,1,0:T(8,128)(2,1)S(1)}, bf16[32,64,256]{2,1,0:T(8,128)(2,1)}, u32[]{:S(2)}) copy-start(bf16[32,64,256]{2,1,0:T(8,128)(2,1)} %basis_hbm.1) | copy-start | bytes 3145732
  4.5 1.2 %copy-start.2 = (f32[32,64,64]{2,1,0:T(8,128)S(1)}, f32[32,64,64]{2,1,0:T(8,128)}, u32[]{:S(2)}) copy-start(f32[32,64,64]{2,1,0:T(8,128)} %transfer_hbm.1) | copy-start | bytes 1572868
  5.7 0.9 %copy-start.3 = (f32[1,6,64,64]{3,2,1,0:T(8,128)S(1)}, f32[1,6,64,64]{3,2,1,0:T(8,128)}, u32[]{:S(2)}) copy-start(f32[1,6,64,64]{3,2,1,0:T(8,128)} %coupling.1) | copy-start | bytes 294916
  6.7 0.9 %copy-start.4 = (f32[1,3,64,64]{3,2,1,0:T(8,128)S(1)}, f32[1,3,64,64]{3,2,1,0:T(8,128)}, u32[]{:S(2)}) copy-start(f32[1,3,64,64]{3,2,1,0:T(8,128)} %branch_tiles.1) | copy-start | bytes 147460
  7.6 0.8 %copy-start.5 = (bf16[3,8192]{1,0:T(4,128)(2,1)S(1)}, bf16[3,8192]{1,0:T(4,128)(2,1)}, u32[]{:S(2)}) copy-start(bf16[3,8192]{1,0:T(4,128)(2,1)} %coords.1) | copy-start | bytes 147460
  8.4 0.8 %copy-start.6 = (f32[1,64,64]{2,1,0:T(8,128)S(1)}, f32[1,64,64]{2,1,0:T(8,128)}, u32[]{:S(2)}) copy-start(f32[1,64,64]{2,1,0:T(8,128)} %cluster_transfer.1) | copy-start | bytes 49156
  9.2 0.7 copy-start.7
  9.8 0.7 copy-start.8
  10.5 0.7 copy-start.9

commit v2 on v1

v2 whole, which is shorter than its diff:
```python
import functools

import jax
import jax.numpy as jnp
from jax import lax
from jax.experimental import pallas as pl
from jax.experimental.pallas import tpu as pltpu
from jax.sharding import PartitionSpec as P

LEAF = 256
RANK = 64
COLS = 64
HERE = 32
NEAR = 5
COUP = 6
BCOUP = 3
REACH = 2
MARGIN = REACH * LEAF
POINTS = HERE * LEAF
PADDED = POINTS + 2 * MARGIN
FEAT = 16

KERNEL_SCALE = 0.03125
DELTA_SQUARED = 0.01

NX, NY = 4, 8
NZ, NC = 8, 2
N_SUB = NX * NY
N_BRANCH = NZ * NC

HIGHEST = lax.Precision.HIGHEST
MESH = pl.DeviceIdType.MESH
F32 = jnp.float32
BF16 = jnp.bfloat16

FIRST_PAIRS = 8


def dot_nn(a, b, precision=None):
    return lax.dot_general(
        a, b, (((1,), (0,)), ((), ())), precision=precision, preferred_element_type=F32
    )


def dot_nt(a, b, precision=None):
    return lax.dot_general(
        a, b, (((1,), (1,)), ((), ())), precision=precision, preferred_element_type=F32
    )


def packed(x):
    half = x.shape[0] // 2
    return jnp.concatenate([x[:half], x[half:]], axis=1)


def unpacked(x):
    half = x.shape[1] // 2
    return jnp.concatenate([x[:, :half], x[:, half:]], axis=0)


def diagonal_blocks(x):
    return x[:RANK, :RANK] + x[RANK:, RANK:]


def features(coords):
    c = coords.astype(F32)
    x, y, z = c[0:1], c[1:2], c[2:3]
    norm = x * x + y * y + z * z + 0.5 * DELTA_SQUARED
    n1 = norm.astype(BF16).astype(F32)
    n2 = (norm - n1).astype(BF16).astype(F32)
    n3 = norm - n1 - n2
    row = lax.broadcasted_iota(jnp.int32, (FEAT, coords.shape[1]), 0)
    ones = jnp.ones_like(norm)

    def stacked(parts):
        out = jnp.zeros((FEAT, coords.shape[1]), F32)
        for at, part in enumerate(parts):
            out = jnp.where(row == at, part, out)
        return out.astype(BF16)

    source = stacked([x, y, z, n1, n2, n3, ones, ones, ones])
    target = stacked([-2.0 * x, -2.0 * y, -2.0 * z, ones, ones, ones, n1, n2, n3])
    return source, target


def leaf_columns(at):
    return pl.ds(pl.multiple_of(at * LEAF, LEAF), LEAF)


def prepare_features(at, coords, source_feat, source_feat_t, target_feat):
    feat_source, feat_target = features(coords[:, leaf_columns(at)])
    source_feat[:, leaf_columns(at + REACH)] = feat_source
    source_feat_t[leaf_columns(at + REACH), :] = feat_source.astype(F32).T.astype(BF16)
    target_feat[:, leaf_columns(at)] = feat_target


def transpose_features(at, source_feat, source_feat_t):
    block = source_feat[:, leaf_columns(at)].astype(F32)
    source_feat_t[leaf_columns(at), :] = block.T.astype(BF16)


def eliminate(k, ref):
    square = ref[:, 0:128]
    lane = lax.broadcasted_iota(jnp.int32, square.shape, 1)
    row = lax.broadcasted_iota(jnp.int32, (RANK, 1), 0)
    column = jnp.sum(jnp.where(lane == k, square, 0.0), axis=1, keepdims=True)
    pivot_row = ref[pl.ds(k, 1), :]
    lane_row = lax.broadcasted_iota(jnp.int32, pivot_row.shape, 1)
    pivot = jnp.sum(jnp.where(lane_row == k, pivot_row, 0.0), axis=1, keepdims=True)
    factor = jnp.where(row > k, column * (1.0 / pivot), 0.0)
    ref[...] = ref[...] - factor * pivot_row


def row_scale(square):
    row = lax.broadcasted_iota(jnp.int32, (RANK, 128), 0)
    lane = lax.broadcasted_iota(jnp.int32, (RANK, 128), 1)
    pivots = jnp.sum(jnp.where(row == lane, square, 0.0), axis=1, keepdims=True)
    return lax.rsqrt(pivots)


def climb_leaves(low, high, total, transfer, basis, window, vt_out):
    def climb(at, total):
        columns = pl.ds(pl.multiple_of(at * LEAF, LEAF), LEAF)
        block = transfer[at].T
        block_high = block.astype(BF16)
        block_low = (block - block_high.astype(F32)).astype(BF16)
        leaf_basis = basis[at]
        vt = (dot_nn(block_high, leaf_basis) + dot_nn(block_low, leaf_basis)).astype(BF16)
        vt_out[:, columns] = vt
        values = window[:, pl.ds(pl.multiple_of(MARGIN + at * LEAF, LEAF), LEAF)]
        return total + dot_nt(vt, jnp.concatenate([vt, values], axis=0))

    return lax.fori_loop(low, high, climb, total, unroll=4)


def near_start(at, made, source_feat_t, target_feat):
    target = target_feat[:, leaf_columns(at)]
    for shift in range(NEAR):
        distance = dot_nn(source_feat_t[leaf_columns(at + shift), :], target)
        made[shift * LEAF : (shift + 1) * LEAF, :] = lax.rsqrt(distance).astype(BF16)


def near_step(at, following, used, made, near_slots, near_count, source_feat_t, target_feat, window, near_out):
    target = target_feat[:, leaf_columns(following)]
    live = near_count[at]
    result = jnp.zeros((COLS, LEAF), F32)
    for shift in range(NEAR):
        weight = jnp.int32(0)
        for slot in range(NEAR):
            weight = weight + jnp.where(
                jnp.logical_and(near_slots[slot, at] == shift, slot < live), 1, 0
            )
        values = window[:, leaf_columns(at + shift)]
        values = values * jnp.full(values.shape, weight.astype(F32)).astype(BF16)
        rows = slice(shift * LEAF, (shift + 1) * LEAF)
        result = result + dot_nn(values, used[rows, :])
        distance = dot_nn(source_feat_t[leaf_columns(following + shift), :], target)
        made[rows, :] = lax.rsqrt(distance).astype(BF16)
    near_out[:, leaf_columns(at)] = result * KERNEL_SCALE


def main_kernel(
    cluster_count,
    branch_count,
    sources,
    coords_hbm,
    basis_hbm,
    transfer_hbm,
    cluster_transfer_hbm,
    near_slots_hbm,
    near_count_hbm,
    cluster_partners_hbm,
    coupling_hbm,
    branch_partners_hbm,
    branch_tiles_hbm,
    near_out,
    vt_out,
    down_out,
    coords,
    basis,
    transfer,
    cluster_transfer,
    near_slots,
    near_count,
    cluster_partners,
    coupling,
    branch_partners,
    branch_tiles,
    window,
    source_feat,
    target_feat,
    source_feat_t,
    all_transfer,
    all_transfer_t,
    all_ortho,
    all_branch,
    left,
    right,
    blocks_even,
    blocks_odd,
    local_sems,
    halo_send,
    halo_recv,
    send_sems,
    recv_sems,
):
    branch = lax.axis_index("branch")
    sub = lax.axis_index("sub")
    sx, sy = sub % NX, sub // NX
    bz, bc = branch // NC, branch % NC

    loads = [
        pltpu.make_async_copy(src, dst, local_sems.at[at])
        for at, (src, dst) in enumerate(
            (
                (transfer_hbm, transfer),
                (basis_hbm, basis),
                (sources, window.at[:, pl.ds(MARGIN, POINTS)]),
                (cluster_transfer_hbm, cluster_transfer),
                (coords_hbm, coords),
                (near_slots_hbm, near_slots),
                (near_count_hbm, near_count),
                (cluster_partners_hbm, cluster_partners),
                (coupling_hbm, coupling),
                (branch_partners_hbm, branch_partners),
                (branch_tiles_hbm, branch_tiles),
            )
        )
    ]
    for load in loads:
        load.start()

    at_x = [(sx + d) % NX for d in range(NX)]
    at_y = [(sy + d) % NY * NX for d in range(NY)]
    at_z = [(bz + d) % NZ * NC for d in range(NZ)]
    at_c = [(bc + d) % NC for d in range(NC)]
    sub_peers = [at_y[o // NX] + at_x[o % NX] for o in range(N_SUB)]
    branch_peers = [at_z[o // NC] + at_c[o % NC] for o in range(N_BRANCH)]

    here = branch * N_SUB + sub
    total = N_BRANCH * N_SUB
    after = (here + 1) % total
    before = (here + total - 1) % total
    after_id = (after // N_SUB, after % N_SUB)
    before_id = (before // N_SUB, before % N_SUB)

    barrier = pltpu.get_barrier_semaphore()
    for device in (
        [(branch, peer) for peer in sub_peers[1:]]
        + [(peer, sub) for peer in branch_peers[1:]]
        + [after_id, before_id]
    ):
        pl.semaphore_signal(barrier, inc=1, device_id=device, device_id_type=MESH)

    def gather_copy(src, dst, slot, device):
        return pltpu.make_async_remote_copy(
            src_ref=src,
            dst_ref=dst,
            send_sem=send_sems.at[slot],
            recv_sem=recv_sems.at[slot],
            device_id=device,
            device_id_type=MESH,
        )

    def all_copies(buffer, slot, count):
        others = buffer.at[pl.ds(1, count - 1)]
        return gather_copy(others, others, slot, (branch, sub_peers[1]))

    def start_sub(buffer, slot):
        for o in range(1, N_SUB):
            gather_copy(buffer.at[0], buffer.at[o], slot, (branch, sub_peers[o])).start()

    def halo_copy(src, dst, at, device):
        return pltpu.make_async_remote_copy(
            src_ref=src,
            dst_ref=dst,
            send_sem=halo_send.at[at],
            recv_sem=halo_recv.at[at],
            device_id=device,
            device_id_type=MESH,
        )

    low, high = pl.ds(0, MARGIN), pl.ds(MARGIN + POINTS, MARGIN)
    halos = [
        halo_copy(
            sources.at[:, pl.ds(POINTS - MARGIN, MARGIN)], window.at[:, low], 0, after_id
        ),
        halo_copy(sources.at[:, pl.ds(0, MARGIN)], window.at[:, high], 1, before_id),
        halo_copy(
            source_feat.at[:, pl.ds(POINTS, MARGIN)], source_feat.at[:, low], 2, after_id
        ),
        halo_copy(
            source_feat.at[:, pl.ds(MARGIN, MARGIN)], source_feat.at[:, high], 3, before_id
        ),
    ]

    for load in loads[:4]:
        load.wait()
    own_transfer = cluster_transfer[0]
    all_transfer[0] = packed(own_transfer).astype(BF16)

    climb = functools.partial(
        climb_leaves, transfer=transfer, basis=basis, window=window, vt_out=vt_out
    )
    gram_up = climb(0, HERE // 2, jnp.zeros((RANK, 2 * RANK), F32))
    pl.semaphore_wait(barrier, N_SUB - 1 + N_BRANCH - 1 + 2)
    start_sub(all_transfer, 0)
    halos[0].start()
    halos[1].start()
    gram_up = climb(HERE // 2, HERE, gram_up)

    row = lax.broadcasted_iota(jnp.int32, (RANK, 128), 0)
    lane = lax.broadcasted_iota(jnp.int32, (RANK, 128), 1)
    identity = jnp.where(row == lane, 1.0, 0.0)
    left[:, 0:128] = gram_up
    left[:, 128:256] = identity
    for load in loads[4:]:
        load.wait()

    @pl.loop(0, HERE)
    def _(it):
        prepare_features(it, coords, source_feat, source_feat_t, target_feat)
        for j in range(RANK // HERE):
            eliminate(it * (RANK // HERE) + j, left)

    scale = row_scale(left[:, 0:128])
    ortho_t = left[:, RANK : 2 * RANK] * scale
    all_ortho[0] = packed(ortho_t).astype(BF16)
    start_sub(all_ortho, 1)
    halos[2].start()
    halos[3].start()

    near_of = dict(
        near_slots=near_slots,
        near_count=near_count,
        source_feat_t=source_feat_t,
        target_feat=target_feat,
        window=window,
        near_out=near_out,
    )
    near_start(REACH, blocks_even, source_feat_t, target_feat)

    def near_pair(at, following):
        near_step(at, at + 1, blocks_even, blocks_odd, **near_of)
        near_step(at + 1, following, blocks_odd, blocks_even, **near_of)

    all_copies(all_transfer, 0, N_SUB).wait_recv()
    stack = all_transfer[...].reshape(N_SUB * RANK // 2, 2 * RANK)
    stack_t = stack.astype(F32).T.astype(BF16)
    all_transfer_t[...] = stack_t
    branch_gram = diagonal_blocks(dot_nn(stack_t, stack))
    right[...] = jnp.concatenate([branch_gram, identity[:, :RANK]], axis=1)

    @pl.loop(0, FIRST_PAIRS)
    def _(it):
        near_pair(REACH + 2 * it, REACH + 2 * it + 2)
        for j in range(RANK // FIRST_PAIRS):
            eliminate(it * (RANK // FIRST_PAIRS) + j, right)

    inverse = left[:, 128 : 128 + RANK] * scale
    inverse_t = inverse.T
    branch_inverse = right[:, RANK:] * row_scale(right[...])

    all_copies(all_ortho, 1, N_SUB).wait_recv()
    branch_up_t = diagonal_blocks(
        dot_nn(all_transfer_t[...], all_ortho[...].reshape(N_SUB * RANK // 2, 2 * RANK))
    )
    branch_ortho_t = dot_nn(branch_inverse, branch_up_t, HIGHEST)
    all_branch[0] = packed(branch_ortho_t).astype(BF16)
    for o in range(1, N_BRANCH):
        gather_copy(all_branch.at[0], all_branch.at[o], 2, (branch_peers[o], sub)).start()

    cluster_map = dot_nt(inverse_t, coupling[0].reshape(COUP * RANK, RANK), HIGHEST)
    handed = dot_nt(dot_nn(inverse_t, own_transfer, HIGHEST), branch_inverse, HIGHEST)
    branch_map = dot_nt(handed, branch_tiles[0].reshape(BCOUP * RANK, RANK), HIGHEST)
    picked = []
    for k in range(COUP):
        partner = cluster_partners[0, k]
        slot = ((sy - partner // NX + NY) % NY) * NX + (sx - partner % NX + NX) % NX
        alive = jnp.where(k < cluster_count[0], 1.0, 0.0)
        picked.append(unpacked(all_ortho[slot].astype(F32)) * alive)
    down_t = dot_nn(cluster_map, jnp.concatenate(picked, axis=0), HIGHEST)

    @pl.loop(FIRST_PAIRS, (HERE - 2 * REACH) // 2)
    def _(it):
        near_pair(
            REACH + 2 * it, jnp.minimum(REACH + 2 * it + 2, HERE - REACH - 1)
        )

    for copy in halos:
        copy.wait_recv()
    keep_low = jnp.where(here == 0, 0.0, 1.0)
    keep_high = jnp.where(here == total - 1, 0.0, 1.0)
    for columns, keep in ((slice(0, MARGIN), keep_low), (slice(MARGIN + POINTS, PADDED), keep_high)):
        edge = window[:, columns]
        window[:, columns] = edge * jnp.full(edge.shape, keep).astype(BF16)
    for at in (0, 1, HERE + REACH, HERE + REACH + 1):
        transpose_features(at, source_feat, source_feat_t)
    near_start(0, blocks_even, source_feat_t, target_feat)
    near_pair(0, HERE - REACH)
    near_pair(HERE - REACH, HERE - 1)

    all_copies(all_branch, 2, N_BRANCH).wait_recv()
    picked = []
    for k in range(BCOUP):
        partner = branch_partners[0, k]
        slot = ((bz - partner // NC + NZ) % NZ) * NC + (bc - partner % NC + NC) % NC
        alive = jnp.where(k < branch_count[0], 1.0, 0.0)
        picked.append(unpacked(all_branch[slot].astype(F32)) * alive)
    down_t = down_t + dot_nn(branch_map, jnp.concatenate(picked, axis=0), HIGHEST)
    down_out[...] = down_t.T

    for copy in halos:
        copy.wait_send()
    all_copies(all_transfer, 0, N_SUB).wait_send()
    all_copies(all_ortho, 1, N_SUB).wait_send()
    all_copies(all_branch, 2, N_BRANCH).wait_send()


def far_kernel(near, vt, down, out):
    high = down[...].astype(BF16)
    low = (down[...] - high.astype(F32)).astype(BF16)
    out[...] = near[...] + dot_nn(high, vt[...]) + dot_nn(low, vt[...])


def shards(
    sources,
    coords,
    leaf_basis,
    leaf_transfer,
    cluster_transfer,
    near_slots,
    near_count,
    cluster_partners,
    cluster_count,
    cluster_coupling,
    branch_partners,
    branch_count,
    branch_coupling_tiles,
):
    vmem = pl.BlockSpec(memory_space=pltpu.VMEM)
    smem = pl.BlockSpec(memory_space=pltpu.SMEM)
    hbm = pl.BlockSpec(memory_space=pltpu.HBM)
    near, vt, down = pl.pallas_call(
        main_kernel,
        out_shape=(
            jax.ShapeDtypeStruct((COLS, POINTS), F32),
            jax.ShapeDtypeStruct((RANK, POINTS), BF16),
            jax.ShapeDtypeStruct((COLS, RANK), F32),
        ),
        in_specs=[smem] * 2 + [hbm] * 11,
        out_specs=(vmem, vmem, vmem),
        scratch_shapes=[
            pltpu.VMEM((3, POINTS), BF16),
            pltpu.VMEM((HERE, RANK, LEAF), BF16),
            pltpu.VMEM((HERE, RANK, RANK), F32),
            pltpu.VMEM((1, RANK, RANK), F32),
            pltpu.SMEM((NEAR, HERE), jnp.int32),
            pltpu.SMEM((HERE,), jnp.int32),
            pltpu.SMEM((1, COUP), jnp.int32),
            pltpu.VMEM((1, COUP, RANK, RANK), F32),
            pltpu.SMEM((1, BCOUP), jnp.int32),
            pltpu.VMEM((1, BCOUP, RANK, RANK), F32),
            pltpu.VMEM((COLS, PADDED), BF16),
            pltpu.VMEM((FEAT, PADDED), BF16),
            pltpu.VMEM((FEAT, POINTS), BF16),
            pltpu.VMEM((PADDED, FEAT), BF16),
            pltpu.VMEM((N_SUB, RANK // 2, 2 * RANK), BF16),
            pltpu.VMEM((2 * RANK, N_SUB * RANK // 2), BF16),
            pltpu.VMEM((N_SUB, RANK // 2, 2 * RANK), BF16),
            pltpu.VMEM((N_BRANCH, RANK // 2, 2 * RANK), BF16),
            pltpu.VMEM((RANK, 256), F32),
            pltpu.VMEM((RANK, 128), F32),
            pltpu.VMEM((NEAR * LEAF, LEAF), BF16),
            pltpu.VMEM((NEAR * LEAF, LEAF), BF16),
            pltpu.SemaphoreType.DMA((11,)),
            pltpu.SemaphoreType.DMA((4,)),
            pltpu.SemaphoreType.DMA((4,)),
            pltpu.SemaphoreType.DMA((3,)),
            pltpu.SemaphoreType.DMA((3,)),
        ],
        compiler_params=pltpu.CompilerParams(
            collective_id=0, has_side_effects=True, vmem_limit_bytes=40 * 2**20
        ),
        name="h2_main",
    )(
        cluster_count,
        branch_count,
        *(
            pltpu.with_memory_space_constraint(operand, pltpu.HBM)
            for operand in (
                sources,
                coords,
                leaf_basis,
                leaf_transfer,
                cluster_transfer,
                near_slots.T,
                near_count,
                cluster_partners,
                cluster_coupling,
                branch_partners,
                branch_coupling_tiles,
            )
        )
    )
    chunk = 2048
    return pl.pallas_call(
        far_kernel,
        out_shape=jax.ShapeDtypeStruct((COLS, POINTS), F32),
        grid=(POINTS // chunk,),
        in_specs=[
            pl.BlockSpec((COLS, chunk), lambda i: (0, i)),
            pl.BlockSpec((RANK, chunk), lambda i: (0, i)),
            pl.BlockSpec((COLS, RANK), lambda i: (0, 0)),
        ],
        out_specs=pl.BlockSpec((COLS, chunk), lambda i: (0, i)),
        compiler_params=pltpu.CompilerParams(vmem_limit_bytes=32 * 2**20),
        name="h2_far",
    )(near, vt, down)


def solution(mesh):
    return jax.shard_map(
        shards,
        mesh=mesh,
        in_specs=(
            P(None, ("branch", "sub")),
            P(None, ("branch", "sub")),
            P(("branch", "sub"), None, None),
            P(("branch", "sub"), None, None),
            P(("branch", "sub"), None, None),
            P(("branch", "sub"), None),
            P(("branch", "sub")),
            P(("branch", "sub"), None),
            P(("branch", "sub")),
            P(("branch", "sub"), None, None, None),
            P("branch", None),
            P("branch"),
            P("branch", None, None, None),
        ),
        out_specs=P(None, ("branch", "sub")),
        check_vma=False,
    )
```

time: 71.4 us -> 45.9 us (0.64)
  Pallas kernels: 59.8 us -> 44.5 us
  local copies, waits for them, and re-layouts: 9.82 us -> 0 us
    pallas_call x1, Pallas kernels: 57.2 us -> 41.9 us  [shards(): pl.pallas_call(main_kernel, out_shape=(jax.ShapeDtypeStruct((COLS, POINTS...]
    unnamed x21 -> x0, local copies, waits for them, and re-layouts: 9.82 us -> none
where the time goes in v2:
time: 45.9 us; the launch traced here: 45.8 us
  Pallas kernels  44.5 us (97%)
  between operations  1.3 us (3%)
    pallas_call x1, Pallas kernels, shards(): pl.pallas_call(main_kernel, out_shape=(jax.ShapeDtypeStruct((COLS, POINTS...  41.9 us
    pallas_call x1, Pallas kernels, shards(): pl.pallas_call(far_kernel, out_shape=jax.ShapeDtypeStruct((COLS, POINTS),...  2.62 us

profile of v2, /device:TPU:1, one launch (start us, length us, event | category | flops | bytes accessed | tf_op | source)
XLA Modules:
  0.0 45.8 jit_solution(17601186979715174252)
XLA Ops:
  1.3 41.9 %h2_main.1 = (f32[64,8192]{1,0:T(8,128)S(1)}, bf16[64,8192]{1,0:T(8,128)(2,1)S(1)}, f32[64,64]{1,0:T(8,128)S(1)}) custom-call(s32[1]{0:T(128)S(6)} %copy.14.cluster_count, s32[1]{0:T(128)S(6)} %copy.15.branch_count, bf16[64,8192]{1,0:T(8,128)(2,1)} %sources.1, bf16[3,8192]{1,0:T(4,128)(2,1)} %coords_hbm.1, bf16[32,64,256]{2,1,0:T(8,128)(2,1)} %basis_hbm.1, ...), custom_call_target="tpu_custom_call" | custom-call | tf_op jit(solution)/shard_map/h2_main/pallas_call | solution.py:444
  43.2 2.6 %h2_far.1 = f32[64,8192]{1,0:T(8,128)} custom-call(f32[64,8192]{1,0:T(8,128)S(1)} %get-tuple-element.8.near, bf16[64,8192]{1,0:T(8,128)(2,1)S(1)} %get-tuple-element.9.vt, f32[64,64]{1,0:T(8,128)S(1)} %get-tuple-element.10.down), custom_call_target="tpu_custom_call" | custom-call | tf_op jit(solution)/shard_map/h2_far/pallas_call | solution.py:507

commit v3 on v2

v3 whole, which is shorter than its diff:
```python
import functools

import jax
import jax.numpy as jnp
from jax import lax
from jax.experimental import pallas as pl
from jax.experimental.pallas import tpu as pltpu
from jax.sharding import PartitionSpec as P

LEAF = 256
RANK = 64
COLS = 64
HERE = 32
NEAR = 5
COUP = 6
BCOUP = 3
REACH = 2
MARGIN = REACH * LEAF
POINTS = HERE * LEAF
PADDED = POINTS + 2 * MARGIN
FEAT = 16

KERNEL_SCALE = 0.03125
DELTA_SQUARED = 0.01

NX, NY = 4, 8
NZ, NC = 8, 2
N_SUB = NX * NY
N_BRANCH = NZ * NC

MESH = pl.DeviceIdType.MESH
F32 = jnp.float32
BF16 = jnp.bfloat16

PAIRS = (2, 6, 11)
FAR = 1024
CLIMB = 16


def dot_nn(a, b, precision=None):
    return lax.dot_general(
        a, b, (((1,), (0,)), ((), ())), precision=precision, preferred_element_type=F32
    )


def dot_nt(a, b, precision=None):
    return lax.dot_general(
        a, b, (((1,), (1,)), ((), ())), precision=precision, preferred_element_type=F32
    )


def halves(x):
    high = x.astype(BF16)
    return high, (x - high.astype(F32)).astype(BF16)


def dot_split(dot, a, b):
    a_high, a_low = halves(a)
    b_high, b_low = halves(b)
    return dot(a_high, b_high) + (dot(a_high, b_low) + dot(a_low, b_high))


def dot_left_split(a, b):
    a_high, a_low = halves(a)
    return dot_nn(a_high, b) + dot_nn(a_low, b)


def packed(x):
    half = x.shape[0] // 2
    return jnp.concatenate([x[:half], x[half:]], axis=1)


def unpacked(x):
    half = x.shape[1] // 2
    return jnp.concatenate([x[:, :half], x[:, half:]], axis=0)


def diagonal_blocks(x):
    return x[:RANK, :RANK] + x[RANK:, RANK:]


def features(coords):
    c = coords.astype(F32)
    x, y, z = c[0:1], c[1:2], c[2:3]
    norm = x * x + y * y + z * z + 0.5 * DELTA_SQUARED
    n1 = norm.astype(BF16).astype(F32)
    n2 = (norm - n1).astype(BF16).astype(F32)
    n3 = norm - n1 - n2
    row = lax.broadcasted_iota(jnp.int32, (FEAT, coords.shape[1]), 0)
    ones = jnp.ones_like(norm)

    def stacked(parts):
        out = jnp.zeros((FEAT, coords.shape[1]), F32)
        for at, part in enumerate(parts):
            out = jnp.where(row == at, part, out)
        return out.astype(BF16)

    source = stacked([x, y, z, n1, n2, n3, ones, ones, ones])
    target = stacked([-2.0 * x, -2.0 * y, -2.0 * z, ones, ones, ones, n1, n2, n3])
    return source, target


def leaf_columns(at):
    return pl.ds(pl.multiple_of(at * LEAF, LEAF), LEAF)


def prepare_features(at, coords, source_feat, source_feat_t, target_feat):
    feat_source, feat_target = features(coords[:, leaf_columns(at)])
    source_feat[:, leaf_columns(at + REACH)] = feat_source
    source_feat_t[leaf_columns(at + REACH), :] = feat_source.astype(F32).T.astype(BF16)
    target_feat[:, leaf_columns(at)] = feat_target


def transpose_features(at, source_feat, source_feat_t):
    block = source_feat[:, leaf_columns(at)].astype(F32)
    source_feat_t[leaf_columns(at), :] = block.T.astype(BF16)


def over_lanes(column):
    return jnp.broadcast_to(column, (column.shape[0], 128))


def eliminate_block(step, ref):
    base = pl.multiple_of(step * 8, 8)
    tiles = [slice(at, at + 128) for at in range(0, ref.shape[1], 128)]
    whole = [ref[:, tile] for tile in tiles]
    rows = [ref[pl.ds(base, 8), tile] for tile in tiles]
    columns = [over_lanes(whole[0][:, j : j + 1]) for j in range(8)]
    heads = [over_lanes(rows[0][:, j : j + 1]) for j in range(8)]
    below = lax.broadcasted_iota(jnp.int32, (RANK, 128), 0) >= base + 8
    sublane = lax.broadcasted_iota(jnp.int32, (8, 128), 0)
    scale = jnp.zeros((8, 128), F32)
    taken = [jnp.zeros((RANK, 128), F32) for _ in tiles]
    for j in range(8):
        pivot = heads[j][j : j + 1, :]
        inverse = 1.0 / pivot
        scale = jnp.where(sublane == j, lax.rsqrt(pivot), scale)
        inside = jnp.where(sublane > j, heads[j] * inverse, 0.0)
        factor = columns[j] * inverse
        for m in range(j + 1, 8):
            entry = heads[m][j : j + 1, :]
            heads[m] = heads[m] - inside * entry
            columns[m] = columns[m] - factor * entry
        for t in range(len(tiles)):
            pivot_row = rows[t][j : j + 1, :]
            rows[t] = rows[t] - inside * pivot_row
            taken[t] = taken[t] + factor * pivot_row
    for t, tile in enumerate(tiles):
        ref[:, tile] = jnp.where(below, whole[t] - taken[t], whole[t])
        ref[pl.ds(base, 8), tile] = rows[t] * scale
    ref[:, 0:128] = pltpu.roll(ref[:, 0:128], 120, 1)


def eliminate(rows):
    sublane = lax.broadcasted_iota(jnp.int32, (8, 128), 0)
    for block in range(RANK // 8):
        lanes = range(8 * block, 8 * block + 8)
        heads = [over_lanes(rows[block][0][:, k : k + 1]) for k in lanes]
        inverses, entries, pivot_rows = [], [], []
        scale = jnp.zeros((8, 128), F32)
        done = rows[block]
        for j in range(8):
            pivot = heads[j][j : j + 1, :]
            inverse = 1.0 / pivot
            scale = jnp.where(sublane == j, lax.rsqrt(pivot), scale)
            inside = jnp.where(sublane > j, heads[j] * inverse, 0.0)
            entry = {m: heads[m][j : j + 1, :] for m in range(j + 1, 8)}
            for m in entry:
                heads[m] = heads[m] - inside * entry[m]
            pivot_row = [tile[j : j + 1, :] for tile in done]
            done = [tile - inside * line for tile, line in zip(done, pivot_row)]
            inverses.append(inverse)
            entries.append(entry)
            pivot_rows.append(pivot_row)
        rows[block] = [tile * scale for tile in done]
        for at in range(block + 1, RANK // 8):
            columns = [over_lanes(rows[at][0][:, k : k + 1]) for k in lanes]
            for j in range(8):
                factor = columns[j] * inverses[j]
                for m, entry in entries[j].items():
                    columns[m] = columns[m] - factor * entry
                rows[at] = [
                    tile - factor * line for tile, line in zip(rows[at], pivot_rows[j])
                ]
    return rows


def climb_leaves(low, high, total, transfer, basis, window, vt_out):
    def lifted(at):
        block = transfer[at].T
        block_high = block.astype(BF16)
        block_low = (block - block_high.astype(F32)).astype(BF16)
        leaf_basis = basis[at]
        return (dot_nn(block_high, leaf_basis) + dot_nn(block_low, leaf_basis)).astype(BF16)

    def climb(it, total):
        points = pl.multiple_of(it * (CLIMB * LEAF), CLIMB * LEAF)
        vt = jnp.concatenate([lifted(it * CLIMB + u) for u in range(CLIMB)], axis=1)
        vt_out[:, pl.ds(points, CLIMB * LEAF)] = vt
        values = window[:, pl.ds(pl.multiple_of(points + MARGIN, LEAF), CLIMB * LEAF)]
        return total + dot_nt(vt, jnp.concatenate([vt, values], axis=0))

    return lax.fori_loop(low // CLIMB, high // CLIMB, climb, total)


def near_start(at, made, source_feat_t, target_feat):
    target = target_feat[:, leaf_columns(at)]
    for shift in range(NEAR):
        distance = dot_nn(source_feat_t[leaf_columns(at + shift), :], target)
        made[shift * LEAF : (shift + 1) * LEAF, :] = lax.rsqrt(distance).astype(BF16)


def near_step(
    at, following, used, made, near_slots, near_count, source_feat_t, target_feat, window, near_out
):
    last = following is None
    target = None if last else target_feat[:, leaf_columns(following)]
    live = near_count[at]
    result = jnp.zeros((COLS, LEAF), F32)
    for shift in range(NEAR):
        weight = jnp.int32(0)
        for slot in range(NEAR):
            weight = weight + jnp.where(
                jnp.logical_and(near_slots[slot, at] == shift, slot < live), 1, 0
            )
        values = window[:, leaf_columns(at + shift)]
        values = values * jnp.full(values.shape, weight.astype(F32)).astype(BF16)
        rows = slice(shift * LEAF, (shift + 1) * LEAF)
        result = result + dot_nn(values, used[rows, :])
        if not last:
            distance = dot_nn(source_feat_t[leaf_columns(following + shift), :], target)
            made[rows, :] = lax.rsqrt(distance).astype(BF16)
    near_out[:, leaf_columns(at)] = result * KERNEL_SCALE


def main_kernel(
    cluster_count,
    branch_count,
    sources,
    coords_hbm,
    basis_hbm,
    transfer_hbm,
    cluster_transfer_hbm,
    near_slots_hbm,
    near_count_hbm,
    cluster_partners_hbm,
    coupling_hbm,
    branch_partners_hbm,
    branch_tiles_hbm,
    near_out,
    vt_out,
    down_out,
    coords,
    basis,
    transfer,
    cluster_transfer,
    near_slots,
    near_count,
    cluster_partners,
    coupling,
    branch_partners,
    branch_tiles,
    window,
    source_feat,
    target_feat,
    source_feat_t,
    all_transfer,
    all_gram,
    all_pairs,
    all_share,
    all_ortho,
    all_branch,
    right,
    blocks_even,
    blocks_odd,
    local_sems,
    halo_send,
    halo_recv,
    send_sems,
    recv_sems,
):
    branch = lax.axis_index("branch")
    sub = lax.axis_index("sub")
    sx, sy = sub % NX, sub // NX
    bz, bc = branch // NC, branch % NC

    half, half_points = HERE // 2, POINTS // 2
    pieces = []
    for part in range(2):
        leaves = pl.ds(part * half, half)
        pieces += [
            (transfer_hbm.at[leaves], transfer.at[leaves]),
            (basis_hbm.at[leaves], basis.at[leaves]),
            (
                sources.at[:, pl.ds(part * half_points, half_points)],
                window.at[:, pl.ds(MARGIN + part * half_points, half_points)],
            ),
        ]
    pieces += [
        (cluster_transfer_hbm, cluster_transfer),
        (coords_hbm, coords),
        (near_slots_hbm, near_slots),
        (near_count_hbm, near_count),
        (cluster_partners_hbm, cluster_partners),
        (coupling_hbm, coupling),
        (branch_partners_hbm, branch_partners),
        (branch_tiles_hbm, branch_tiles),
    ]
    loads = [
        pltpu.make_async_copy(src, dst, local_sems.at[at])
        for at, (src, dst) in enumerate(pieces)
    ]
    for load in loads:
        load.start()

    at_x = [(sx + d) % NX for d in range(NX)]
    at_y = [(sy + d) % NY * NX for d in range(NY)]
    at_z = [(bz + d) % NZ * NC for d in range(NZ)]
    at_c = [(bc + d) % NC for d in range(NC)]
    peers_x = [(branch, at_y[0] + at_x[d]) for d in range(NX)]
    peers_y = [(branch, at_y[d] + at_x[0]) for d in range(NY)]
    peers_z = [(at_z[d] + at_c[0], sub) for d in range(NZ)]
    peer_core = (at_z[0] + at_c[1], sub)

    here = branch * N_SUB + sub
    total = N_BRANCH * N_SUB
    after = (here + 1) % total
    before = (here + total - 1) % total
    after_id = (after // N_SUB, after % N_SUB)
    before_id = (before // N_SUB, before % N_SUB)

    barrier = pltpu.get_barrier_semaphore()
    greeted = peers_z[1:] + peers_y[1:] + peers_x[1:] + [peer_core, after_id, before_id]
    for device in greeted:
        pl.semaphore_signal(barrier, inc=1, device_id=device, device_id_type=MESH)

    def gather_copy(src, dst, slot, device):
        return pltpu.make_async_remote_copy(
            src_ref=src,
            dst_ref=dst,
            send_sem=send_sems.at[slot],
            recv_sem=recv_sems.at[slot],
            device_id=device,
            device_id_type=MESH,
        )

    def all_copies(buffer, slot, count, first=1):
        others = buffer.at[pl.ds(first, count - first)]
        return gather_copy(others, others, slot, peer_core)

    def start_ring(buffer, slot, peers, width=1):
        size = len(peers)
        for d in sorted(range(1, size), key=lambda d: -min(d, size - d)):
            gather_copy(
                buffer.at[pl.ds(0, width)],
                buffer.at[pl.ds(d * width, width)],
                slot,
                peers[d],
            ).start()

    def halo_copy(src, dst, at, device):
        return pltpu.make_async_remote_copy(
            src_ref=src,
            dst_ref=dst,
            send_sem=halo_send.at[at],
            recv_sem=halo_recv.at[at],
            device_id=device,
            device_id_type=MESH,
        )

    low, high = pl.ds(0, MARGIN), pl.ds(MARGIN + POINTS, MARGIN)
    halos = [
        halo_copy(
            sources.at[:, pl.ds(POINTS - MARGIN, MARGIN)], window.at[:, low], 0, after_id
        ),
        halo_copy(sources.at[:, pl.ds(0, MARGIN)], window.at[:, high], 1, before_id),
        halo_copy(
            source_feat.at[:, pl.ds(POINTS, MARGIN)], source_feat.at[:, low], 2, after_id
        ),
        halo_copy(
            source_feat.at[:, pl.ds(MARGIN, MARGIN)], source_feat.at[:, high], 3, before_id
        ),
    ]

    climb = functools.partial(
        climb_leaves, transfer=transfer, basis=basis, window=window, vt_out=vt_out
    )
    for load in loads[:3]:
        load.wait()
    gram_up = climb(0, half, jnp.zeros((RANK, 2 * RANK), F32))

    loads[6].wait()
    own_transfer = cluster_transfer[0]
    all_transfer[0] = packed(own_transfer).astype(BF16)
    own_transfer_t = own_transfer.T.astype(BF16)
    pl.semaphore_wait(barrier, len(greeted))
    start_ring(all_transfer, 0, peers_x)
    halos[0].start()
    halos[1].start()

    for load in loads[3:6]:
        load.wait()
    gram_up = climb(half, HERE, gram_up)

    row = lax.broadcasted_iota(jnp.int32, (RANK, 128), 0)
    lane = lax.broadcasted_iota(jnp.int32, (RANK, 128), 1)
    identity = jnp.where(row == lane, 1.0, 0.0)
    rows = eliminate(
        [[part[8 * r : 8 * r + 8, :] for part in (gram_up, identity)] for r in range(RANK // 8)]
    )
    ortho_t = jnp.concatenate([tiles[0][:, RANK:] for tiles in rows], axis=0)
    inverse = jnp.concatenate([tiles[1][:, :RANK] for tiles in rows], axis=0)
    share = dot_nn(own_transfer_t, ortho_t.astype(BF16))
    all_pairs[0] = jnp.concatenate([packed(share), packed(ortho_t)], axis=0).astype(BF16)
    start_ring(all_pairs, 1, peers_x)

    all_copies(all_transfer, 0, NX).wait_recv()
    stack = all_transfer[...].reshape(NX * RANK // 2, 2 * RANK)
    partial_gram = diagonal_blocks(dot_nn(stack.astype(F32).T.astype(BF16), stack))
    all_gram[0] = packed(partial_gram).astype(BF16)
    start_ring(all_gram, 3, peers_y)

    near_of = dict(
        near_slots=near_slots,
        near_count=near_count,
        source_feat_t=source_feat_t,
        target_feat=target_feat,
        window=window,
        near_out=near_out,
    )

    def prepare(at):
        prepare_features(at, coords, source_feat, source_feat_t, target_feat)

    for load in loads[7:]:
        load.wait()
    for at in (0, 1, HERE - 2, HERE - 1):
        prepare(at)
    halos[2].start()
    halos[3].start()
    for at in range(REACH, 2 * REACH + 2):
        prepare(at)
    near_start(REACH, blocks_even, source_feat_t, target_feat)

    def near_pair(at, following):
        for step, used, made in ((0, blocks_even, blocks_odd), (1, blocks_odd, blocks_even)):
            prepare(jnp.minimum(at + step + 2 * REACH, HERE - REACH - 1))
            near_step(at + step, following if step else at + 1, used, made, **near_of)

    inverse_t = inverse.T
    all_copies(all_pairs, 1, NX).wait_recv()
    pairs = all_pairs[...]
    all_share[0] = jnp.sum(pairs[:, : RANK // 2].astype(F32), axis=0).astype(BF16)
    start_ring(all_share, 4, peers_y)
    all_ortho[0:NX] = pairs[:, RANK // 2 :]
    start_ring(all_ortho, 5, peers_y, NX)

    def plain_pairs(first, last):
        @pl.loop(first, last)
        def _(it):
            near_pair(REACH + 2 * it, REACH + 2 * it + 2)

    plain_pairs(0, PAIRS[0])
    all_copies(all_gram, 3, NY).wait_recv()
    branch_gram = unpacked(jnp.sum(all_gram[...].astype(F32), axis=0))
    right[...] = jnp.concatenate([branch_gram, identity[:, :RANK]], axis=1)

    @pl.loop(PAIRS[0], PAIRS[1])
    def _(it):
        near_pair(REACH + 2 * it, REACH + 2 * it + 2)
        blocks = RANK // 8 // (PAIRS[1] - PAIRS[0])
        for j in range(blocks):
            eliminate_block((it - PAIRS[0]) * blocks + j, right)

    branch_inverse = right[:, 0:RANK]

    all_copies(all_share, 4, NY).wait_recv()
    branch_up_t = unpacked(jnp.sum(all_share[...].astype(F32), axis=0))
    branch_ortho_t = dot_split(dot_nn, branch_inverse, branch_up_t)
    all_branch[0] = packed(branch_ortho_t).astype(BF16)
    start_ring(all_branch, 2, peers_z)

    cluster_map = dot_split(dot_nt, inverse_t, coupling[0].reshape(COUP * RANK, RANK))
    handed = dot_split(dot_nt, dot_split(dot_nn, inverse_t, own_transfer), branch_inverse)
    branch_map = dot_split(dot_nt, handed, branch_tiles[0].reshape(BCOUP * RANK, RANK))

    plain_pairs(PAIRS[1], PAIRS[2])

    all_copies(all_branch, 2, NZ).wait_recv()
    gather_copy(
        all_branch.at[pl.ds(0, NZ)], all_branch.at[pl.ds(NZ, NZ)], 6, peer_core
    ).start()

    plain_pairs(PAIRS[2], (HERE - 2 * REACH) // 2 - 1)
    for copy in halos:
        copy.wait_recv()
    keep_low = jnp.where(here == 0, 0.0, 1.0)
    keep_high = jnp.where(here == total - 1, 0.0, 1.0)
    for columns, keep in ((slice(0, MARGIN), keep_low), (slice(MARGIN + POINTS, PADDED), keep_high)):
        edge = window[:, columns]
        window[:, columns] = edge * jnp.full(edge.shape, keep).astype(BF16)
    for at in (0, 1, HERE + REACH, HERE + REACH + 1):
        transpose_features(at, source_feat, source_feat_t)
    edges = (HERE - REACH - 2, HERE - REACH - 1, 0, 1, HERE - 2, HERE - 1, None)
    for it in range(6):
        used, made = ((blocks_even, blocks_odd), (blocks_odd, blocks_even))[it % 2]
        near_step(edges[it], edges[it + 1], used, made, **near_of)

    all_copies(all_ortho, 5, N_SUB, NX).wait_recv()
    picked = []
    for k in range(COUP):
        partner = cluster_partners[0, k]
        slot = ((sy - partner // NX + NY) % NY) * NX + (sx - partner % NX + NX) % NX
        alive = jnp.where(k < cluster_count[0], 1.0, 0.0)
        picked.append((unpacked(all_ortho[slot].astype(F32)) * alive).astype(BF16))
    down_t = dot_left_split(cluster_map, jnp.concatenate(picked, axis=0))

    all_copies(all_branch, 6, 2 * NZ, NZ).wait_recv()
    picked = []
    for k in range(BCOUP):
        partner = branch_partners[0, k]
        slot = ((bc - partner % NC + NC) % NC) * NZ + (bz - partner // NC + NZ) % NZ
        alive = jnp.where(k < branch_count[0], 1.0, 0.0)
        picked.append((unpacked(all_branch[slot].astype(F32)) * alive).astype(BF16))
    down_t = down_t + dot_left_split(branch_map, jnp.concatenate(picked, axis=0))
    down_out[...] = down_t.T

    for copy in halos:
        copy.wait_send()
    all_copies(all_transfer, 0, NX).wait_send()
    all_copies(all_pairs, 1, NX).wait_send()
    all_copies(all_branch, 2, NZ).wait_send()
    all_copies(all_gram, 3, NY).wait_send()
    all_copies(all_share, 4, NY).wait_send()
    all_copies(all_ortho, 5, N_SUB, NX).wait_send()
    all_copies(all_branch, 6, 2 * NZ, NZ).wait_send()


def far_kernel(near, vt, down, out, total, sems):
    high = down[...].astype(BF16)
    low = (down[...] - high.astype(F32)).astype(BF16)
    copies = []
    for at in range(POINTS // FAR):
        columns = slice(at * FAR, (at + 1) * FAR)
        total[:, columns] = (
            near[:, columns] + dot_nn(high, vt[:, columns]) + dot_nn(low, vt[:, columns])
        )
        copies.append(
            pltpu.make_async_copy(total.at[:, columns], out.at[:, columns], sems.at[at])
        )
        copies[-1].start()
    for copy in copies:
        copy.wait()


def shards(
    sources,
    coords,
    leaf_basis,
    leaf_transfer,
    cluster_transfer,
    near_slots,
    near_count,
    cluster_partners,
    cluster_count,
    cluster_coupling,
    branch_partners,
    branch_count,
    branch_coupling_tiles,
):
    vmem = pl.BlockSpec(memory_space=pltpu.VMEM)
    smem = pl.BlockSpec(memory_space=pltpu.SMEM)
    hbm = pl.BlockSpec(memory_space=pltpu.HBM)
    near, vt, down = pl.pallas_call(
        main_kernel,
        out_shape=(
            jax.ShapeDtypeStruct((COLS, POINTS), F32),
            jax.ShapeDtypeStruct((RANK, POINTS), BF16),
            jax.ShapeDtypeStruct((COLS, RANK), F32),
        ),
        in_specs=[smem] * 2 + [hbm] * 11,
        out_specs=(vmem, vmem, vmem),
        scratch_shapes=[
            pltpu.VMEM((3, POINTS), BF16),
            pltpu.VMEM((HERE, RANK, LEAF), BF16),
            pltpu.VMEM((HERE, RANK, RANK), F32),
            pltpu.VMEM((1, RANK, RANK), F32),
            pltpu.SMEM((NEAR, HERE), jnp.int32),
            pltpu.SMEM((HERE,), jnp.int32),
            pltpu.SMEM((1, COUP), jnp.int32),
            pltpu.VMEM((1, COUP, RANK, RANK), F32),
            pltpu.SMEM((1, BCOUP), jnp.int32),
            pltpu.VMEM((1, BCOUP, RANK, RANK), F32),
            pltpu.VMEM((COLS, PADDED), BF16),
            pltpu.VMEM((FEAT, PADDED), BF16),
            pltpu.VMEM((FEAT, POINTS), BF16),
            pltpu.VMEM((PADDED, FEAT), BF16),
            pltpu.VMEM((NX, RANK // 2, 2 * RANK), BF16),
            pltpu.VMEM((NY, RANK // 2, 2 * RANK), BF16),
            pltpu.VMEM((NX, RANK, 2 * RANK), BF16),
            pltpu.VMEM((NY, RANK // 2, 2 * RANK), BF16),
            pltpu.VMEM((N_SUB, RANK // 2, 2 * RANK), BF16),
            pltpu.VMEM((N_BRANCH, RANK // 2, 2 * RANK), BF16),
            pltpu.VMEM((RANK, 128), F32),
            pltpu.VMEM((NEAR * LEAF, LEAF), BF16),
            pltpu.VMEM((NEAR * LEAF, LEAF), BF16),
            pltpu.SemaphoreType.DMA((14,)),
            pltpu.SemaphoreType.DMA((4,)),
            pltpu.SemaphoreType.DMA((4,)),
            pltpu.SemaphoreType.DMA((7,)),
            pltpu.SemaphoreType.DMA((7,)),
        ],
        compiler_params=pltpu.CompilerParams(
            collective_id=0, has_side_effects=True, vmem_limit_bytes=40 * 2**20
        ),
        name="h2_main",
    )(
        cluster_count,
        branch_count,
        *(
            pltpu.with_memory_space_constraint(operand, pltpu.HBM)
            for operand in (
                sources,
                coords,
                leaf_basis,
                leaf_transfer,
                cluster_transfer,
                near_slots.T,
                near_count,
                cluster_partners,
                cluster_coupling,
                branch_partners,
                branch_coupling_tiles,
            )
        )
    )
    return pl.pallas_call(
        far_kernel,
        out_shape=jax.ShapeDtypeStruct((COLS, POINTS), F32),
        in_specs=[vmem] * 3,
        out_specs=hbm,
        scratch_shapes=[
            pltpu.VMEM((COLS, POINTS), F32),
            pltpu.SemaphoreType.DMA((POINTS // FAR,)),
        ],
        compiler_params=pltpu.CompilerParams(vmem_limit_bytes=32 * 2**20),
        name="h2_far",
    )(near, vt, down)


def solution(mesh):
    return jax.shard_map(
        shards,
        mesh=mesh,
        in_specs=(
            P(None, ("branch", "sub")),
            P(None, ("branch", "sub")),
            P(("branch", "sub"), None, None),
            P(("branch", "sub"), None, None),
            P(("branch", "sub"), None, None),
            P(("branch", "sub"), None),
            P(("branch", "sub")),
            P(("branch", "sub"), None),
            P(("branch", "sub")),
            P(("branch", "sub"), None, None, None),
            P("branch", None),
            P("branch"),
            P("branch", None, None, None),
        ),
        out_specs=P(None, ("branch", "sub")),
        check_vma=False,
    )
```

time: 45.9 us -> 38.2 us (0.83); the launches traced: 45.8 us -> 37.6 us
  Pallas kernels: 44.5 us -> 36.3 us
    pallas_call x1, Pallas kernels: 41.9 us -> 34.7 us  [shards(): pl.pallas_call(main_kernel, out_shape=(jax.ShapeDtypeStruct((COLS, POINTS...]
    pallas_call x1, Pallas kernels: 2.62 us -> 1.59 us  [shards(): pl.pallas_call(far_kernel, out_shape=jax.ShapeDtypeStruct((COLS, POINTS),...]
where the time goes in v3:
time: 38.2 us; the launch traced here: 37.6 us
  Pallas kernels  36.3 us (95%)
  between operations  1.3 us (3%)
    pallas_call x1, Pallas kernels, shards(): pl.pallas_call(main_kernel, out_shape=(jax.ShapeDtypeStruct((COLS, POINTS...  34.7 us
    pallas_call x1, Pallas kernels, shards(): pl.pallas_call(far_kernel, out_shape=jax.ShapeDtypeStruct((COLS, POINTS),...  1.59 us

profile of v3, /device:TPU:1, one launch (start us, length us, event | category | flops | bytes accessed | tf_op | source)
XLA Modules:
  0.0 37.6 jit_solution(1039625423096858483)
XLA Ops:
  1.3 34.7 %h2_main.1 = (f32[64,8192]{1,0:T(8,128)S(1)}, bf16[64,8192]{1,0:T(8,128)(2,1)S(1)}, f32[64,64]{1,0:T(8,128)S(1)}) custom-call(s32[1]{0:T(128)S(6)} %copy.14.cluster_count, s32[1]{0:T(128)S(6)} %copy.15.branch_count, bf16[64,8192]{1,0:T(8,128)(2,1)} %sources.1, bf16[3,8192]{1,0:T(4,128)(2,1)} %coords_hbm.1, bf16[32,64,256]{2,1,0:T(8,128)(2,1)} %basis_hbm.1, ...), custom_call_target="tpu_custom_call" | custom-call | tf_op jit(solution)/shard_map/h2_main/pallas_call | solution.py:574
  36.0 1.6 %h2_far.1 = f32[64,8192]{1,0:T(8,128)} custom-call(f32[64,8192]{1,0:T(8,128)S(1)} %get-tuple-element.8.near, bf16[64,8192]{1,0:T(8,128)(2,1)S(1)} %get-tuple-element.9.vt, f32[64,64]{1,0:T(8,128)S(1)} %get-tuple-element.10.down), custom_call_target="tpu_custom_call" | custom-call | tf_op jit(solution)/shard_map/h2_far/pallas_call | solution.py:637

commit v4 on v3

--- a/solution.py
+++ b/solution.py
@@ -32,7 +32,7 @@
 F32 = jnp.float32
 BF16 = jnp.bfloat16
 
-PAIRS = (2, 6, 11)
+PAIRS = (0, 2, 6, 12)
 FAR = 1024
 CLIMB = 16
 
@@ -86,18 +86,17 @@
     n1 = norm.astype(BF16).astype(F32)
     n2 = (norm - n1).astype(BF16).astype(F32)
     n3 = norm - n1 - n2
-    row = lax.broadcasted_iota(jnp.int32, (FEAT, coords.shape[1]), 0)
-    ones = jnp.ones_like(norm)
-
-    def stacked(parts):
-        out = jnp.zeros((FEAT, coords.shape[1]), F32)
-        for at, part in enumerate(parts):
-            out = jnp.where(row == at, part, out)
-        return out.astype(BF16)
-
-    source = stacked([x, y, z, n1, n2, n3, ones, ones, ones])
-    target = stacked([-2.0 * x, -2.0 * y, -2.0 * z, ones, ones, ones, n1, n2, n3])
-    return source, target
+    row = lax.broadcasted_iota(jnp.int32, (FEAT // 2, coords.shape[1]), 0)
+    point = jnp.zeros((FEAT // 2, coords.shape[1]), F32)
+    for at, part in enumerate((x, y, z, n1, n2, n3)):
+        point = jnp.where(row == at, part, point)
+    is_norm = jnp.logical_and(row >= 3, row < 6)
+    ones = jnp.where(is_norm, 1.0, 0.0)
+    source = jnp.concatenate([point, ones], axis=0)
+    target = jnp.concatenate(
+        [jnp.where(is_norm, 1.0, -2.0 * point), jnp.where(is_norm, point, 0.0)], axis=0
+    )
+    return source, target.astype(BF16)
 
 
 def leaf_columns(at):
@@ -106,8 +105,8 @@
 
 def prepare_features(at, coords, source_feat, source_feat_t, target_feat):
     feat_source, feat_target = features(coords[:, leaf_columns(at)])
-    source_feat[:, leaf_columns(at + REACH)] = feat_source
-    source_feat_t[leaf_columns(at + REACH), :] = feat_source.astype(F32).T.astype(BF16)
+    source_feat[:, leaf_columns(at + REACH)] = feat_source.astype(BF16)
+    source_feat_t[leaf_columns(at + REACH), :] = feat_source.T.astype(BF16)
     target_feat[:, leaf_columns(at)] = feat_target
 
 
@@ -447,6 +446,12 @@
             prepare(jnp.minimum(at + step + 2 * REACH, HERE - REACH - 1))
             near_step(at + step, following if step else at + 1, used, made, **near_of)
 
+    def plain_pairs(first, last):
+        @pl.loop(first, last, unroll=2 - (last - first) % 2)
+        def _(it):
+            near_pair(REACH + 2 * it, REACH + 2 * it + 2)
+
+    plain_pairs(0, PAIRS[0])
     inverse_t = inverse.T
     all_copies(all_pairs, 1, NX).wait_recv()
     pairs = all_pairs[...]
@@ -455,22 +460,17 @@
     all_ortho[0:NX] = pairs[:, RANK // 2 :]
     start_ring(all_ortho, 5, peers_y, NX)
 
-    def plain_pairs(first, last):
-        @pl.loop(first, last)
-        def _(it):
-            near_pair(REACH + 2 * it, REACH + 2 * it + 2)
-
-    plain_pairs(0, PAIRS[0])
+    plain_pairs(PAIRS[0], PAIRS[1])
     all_copies(all_gram, 3, NY).wait_recv()
     branch_gram = unpacked(jnp.sum(all_gram[...].astype(F32), axis=0))
     right[...] = jnp.concatenate([branch_gram, identity[:, :RANK]], axis=1)
 
-    @pl.loop(PAIRS[0], PAIRS[1])
+    @pl.loop(PAIRS[1], PAIRS[2], unroll=2)
     def _(it):
         near_pair(REACH + 2 * it, REACH + 2 * it + 2)
-        blocks = RANK // 8 // (PAIRS[1] - PAIRS[0])
+        blocks = RANK // 8 // (PAIRS[2] - PAIRS[1])
         for j in range(blocks):
-            eliminate_block((it - PAIRS[0]) * blocks + j, right)
+            eliminate_block((it - PAIRS[1]) * blocks + j, right)
 
     branch_inverse = right[:, 0:RANK]
 
@@ -484,14 +484,14 @@
     handed = dot_split(dot_nt, dot_split(dot_nn, inverse_t, own_transfer), branch_inverse)
     branch_map = dot_split(dot_nt, handed, branch_tiles[0].reshape(BCOUP * RANK, RANK))
 
-    plain_pairs(PAIRS[1], PAIRS[2])
+    plain_pairs(PAIRS[2], PAIRS[3])
 
     all_copies(all_branch, 2, NZ).wait_recv()
     gather_copy(
         all_branch.at[pl.ds(0, NZ)], all_branch.at[pl.ds(NZ, NZ)], 6, peer_core
     ).start()
 
-    plain_pairs(PAIRS[2], (HERE - 2 * REACH) // 2 - 1)
+    plain_pairs(PAIRS[3], (HERE - 2 * REACH) // 2 - 1)
     for copy in halos:
         copy.wait_recv()
     keep_low = jnp.where(here == 0, 0.0, 1.0)

time: 38.2 us -> 37.7 us (0.987); the launches traced: 37.6 us -> 37.5 us
  no operation moved by 1% of the time
where the time goes in v4:
time: 37.7 us; the launch traced here: 37.5 us
  Pallas kernels  36.2 us (96%)
  between operations  1.3 us (3%)
    pallas_call x1, Pallas kernels, shards(): pl.pallas_call(main_kernel, out_shape=(jax.ShapeDtypeStruct((COLS, POINTS...  34.6 us
    pallas_call x1, Pallas kernels, shards(): pl.pallas_call(far_kernel, out_shape=jax.ShapeDtypeStruct((COLS, POINTS),...  1.59 us

profile of v4, /device:TPU:1, one launch (start us, length us, event | category | flops | bytes accessed | tf_op | source)
XLA Modules:
  0.0 37.5 jit_solution(8141038641199233002)
XLA Ops:
  1.3 34.6 %h2_main.1 = (f32[64,8192]{1,0:T(8,128)S(1)}, bf16[64,8192]{1,0:T(8,128)(2,1)S(1)}, f32[64,64]{1,0:T(8,128)S(1)}) custom-call(s32[1]{0:T(128)S(6)} %copy.14.cluster_count, s32[1]{0:T(128)S(6)} %copy.15.branch_count, bf16[64,8192]{1,0:T(8,128)(2,1)} %sources.1, bf16[3,8192]{1,0:T(4,128)(2,1)} %coords_hbm.1, bf16[32,64,256]{2,1,0:T(8,128)(2,1)} %basis_hbm.1, ...), custom_call_target="tpu_custom_call" | custom-call | tf_op jit(solution)/shard_map/h2_main/pallas_call | solution.py:574
  35.9 1.6 %h2_far.1 = f32[64,8192]{1,0:T(8,128)} custom-call(f32[64,8192]{1,0:T(8,128)S(1)} %get-tuple-element.8.near, bf16[64,8192]{1,0:T(8,128)(2,1)S(1)} %get-tuple-element.9.vt, f32[64,64]{1,0:T(8,128)S(1)} %get-tuple-element.10.down), custom_call_target="tpu_custom_call" | custom-call | tf_op jit(solution)/shard_map/h2_far/pallas_call | solution.py:637
